TPU v7x, 32 devices: a whole 2x2x4 slice. The times are simulated.
32 devices in a mesh: dp: 4 (over x, core), mem: 8 (over z, y).
Axes of the slice: x: 2, y: 2, z: 4, core: 2. Of those that a mesh axis runs over, the one named last changes fastest.
Arguments:
- tokens: bfloat16 [4096, 2048], P(('dp', 'mem')), may hold values from -60 to 60
- norm_gain: float32 [2048], replicated, may hold values from 0.1 to 1.9
- query_weight: bfloat16 [2048, 2048], P(None, 'dp'), may hold values from -0.125 to 0.125
- values: bfloat16 [32768, 2048], P(('dp', 'mem')), may hold values from -6 to 6
- blocks: int32 [4096, 2], P(('dp', 'mem')), may hold values from 0 to 511, as said below
- weights: float32 [4096, 2], P(('dp', 'mem')), may hold values from 0.25 to 1
- out_cotangent: bfloat16 [4096, 2048], P(('dp', 'mem')), may hold values from -6 to 6
Outputs:
- layer_out: float32 [4096, 2048], P(('dp', 'mem'))
- grad_tokens: float32 [4096, 2048], P(('dp', 'mem'))
- grad_values: bfloat16 [32768, 2048], P(('dp', 'mem'))
Inputs may be any that keep to these rules, and one draw needn't show every extreme that they name: Block b is held by device b // 16, devices counted as the tokens are (dp major, mem minor). The 2 blocks of one token differ. The tokens of one device make at most 16 lookups (repeats counted) into the blocks held by any one device, and in every draw some devices receive exactly 16 lookups from the tokens of every device.
All inputs are finite; a program needn't handle non-finite values.
Results may differ from a plain program's by a relative error of at most 0.012.
Values may be sent and summed in bfloat16 or wider, within the bound.
A program may use at most 128 MiB of HBM per device.

v0:
```python
import jax
import jax.numpy as jnp
from jax import lax
from jax.sharding import PartitionSpec as P

BLOCK = 64


def against_rows(left, table):
    return lax.dot_general(
        left, table, (((1,), (1,)), ((), ())), preferred_element_type=jnp.float32
    )


def over_slots(left, right):
    return lax.dot_general(
        left, right, (((0,), (0,)), ((), ())), preferred_element_type=jnp.float32
    )


def serve_lookups(payload, block_ids, values, features):
    owner_count, slot_count = block_ids.shape
    value_rows = values.shape[0]
    score_scale = float(features) ** (-0.5)
    flat_load = payload.reshape(owner_count * slot_count, 2 * features)
    query_rows = flat_load[:, :features]
    cot_rows = flat_load[:, features:]
    row_block = jnp.arange(value_rows, dtype=jnp.int32) // BLOCK
    in_block = block_ids.reshape(owner_count * slot_count)[:, None] == row_block[None, :]
    scores = against_rows(query_rows, values) * score_scale
    sigmoid_of = jax.nn.sigmoid(scores)
    gate_values = jnp.where(in_block, sigmoid_of, 0.0).astype(jnp.bfloat16)
    block_parts = jnp.dot(gate_values, values, preferred_element_type=jnp.float32).astype(
        jnp.bfloat16
    )
    cot_scores = against_rows(cot_rows, values)
    score_grads = jnp.where(
        in_block, cot_scores * sigmoid_of * (1.0 - sigmoid_of) * score_scale, 0.0
    ).astype(jnp.bfloat16)
    query_parts = jnp.dot(score_grads, values, preferred_element_type=jnp.float32).astype(
        jnp.bfloat16
    )
    answer = jnp.concatenate([block_parts, query_parts], axis=1).reshape(
        owner_count, slot_count, 2 * features
    )
    return (
        answer,
        gate_values.reshape(owner_count, slot_count, value_rows),
        score_grads.reshape(owner_count, slot_count, value_rows),
    )


def body(tokens, norm_gain, query_weight, values, blocks, weights, out_cotangent):
    token_count, features = tokens.shape
    top_count = blocks.shape[1]
    value_rows = values.shape[0]
    span_blocks = value_rows // BLOCK
    dp_count = lax.axis_size("dp")
    mem_count = lax.axis_size("mem")
    owner_count = dp_count * mem_count
    pair_count = token_count * top_count
    capacity = 2 * pair_count // owner_count
    weight_full = lax.all_gather(query_weight, "dp", axis=1, tiled=True)
    exact_tokens = tokens.astype(jnp.float32)
    rms_rows = lax.rsqrt(jnp.mean(exact_tokens * exact_tokens, axis=1, keepdims=True) + 1e-06)
    unit_rows = exact_tokens * rms_rows
    normed = (unit_rows * norm_gain).astype(jnp.bfloat16)
    queries = jnp.dot(normed, weight_full, preferred_element_type=jnp.float32).astype(jnp.bfloat16)
    scaled_cot = (weights[:, :, None] * out_cotangent.astype(jnp.float32)[:, None, :]).astype(
        jnp.bfloat16
    )
    flat_ids = blocks.reshape(pair_count)
    owner_of = flat_ids // span_blocks
    local_block = flat_ids % span_blocks
    owner_hits = (owner_of[:, None] == jnp.arange(owner_count, dtype=jnp.int32)[None, :]).astype(
        jnp.int32
    )
    slot_of = jnp.sum((jnp.cumsum(owner_hits, axis=0) - 1) * owner_hits, axis=1)
    target = owner_of * capacity + slot_of
    source_of = (
        jnp.full((owner_count * capacity,), pair_count, jnp.int32)
        .at[target]
        .set(jnp.arange(pair_count, dtype=jnp.int32))
    )
    query_pairs = jnp.broadcast_to(queries[:, None, :], (token_count, top_count, features))
    pair_load = jnp.concatenate([query_pairs, scaled_cot], axis=2).reshape(pair_count, 2 * features)
    pair_load = jnp.concatenate([pair_load, jnp.zeros((1, 2 * features), jnp.bfloat16)], axis=0)
    payload = pair_load[source_of].reshape(owner_count, capacity, 2 * features)
    padded_ids = jnp.concatenate([local_block, jnp.full((1,), -1, jnp.int32)], axis=0)
    slot_ids = padded_ids[source_of].reshape(owner_count, capacity)
    pieces = (
        lax.all_to_all(payload, ("dp", "mem"), split_axis=0, concat_axis=0, tiled=True),
        lax.all_to_all(slot_ids, ("dp", "mem"), split_axis=0, concat_axis=0, tiled=True),
    )
    answer, gate_values, score_grads = serve_lookups(pieces[0], pieces[1], values, features)
    returned = lax.all_to_all(answer, ("dp", "mem"), split_axis=0, concat_axis=0, tiled=True)
    returned, gate_values, score_grads, received = (returned, gate_values, score_grads, pieces[0])
    slot_total = owner_count * capacity
    received_flat = received.reshape(slot_total, 2 * features)
    grad_sum = over_slots(gate_values.reshape(slot_total, value_rows), received_flat[:, features:])
    grad_sum = grad_sum + over_slots(
        score_grads.reshape(slot_total, value_rows), received_flat[:, :features]
    )
    grad_values = grad_sum.astype(jnp.bfloat16)
    answers = returned.reshape(slot_total, 2 * features)[target].reshape(
        token_count, top_count, 2 * features
    )
    block_parts = answers[:, :, :features].astype(jnp.float32)
    query_parts = answers[:, :, features:].astype(jnp.float32)
    layer_out = exact_tokens + jnp.sum(weights[:, :, None] * block_parts, axis=1)
    query_grad = jnp.sum(query_parts, axis=1).astype(jnp.bfloat16)
    normed_grad = against_rows(query_grad, weight_full)
    unit_grad = normed_grad * norm_gain
    grad_tokens = out_cotangent.astype(jnp.float32) + rms_rows * (
        unit_grad - unit_rows * jnp.mean(unit_grad * unit_rows, axis=1, keepdims=True)
    )
    return (layer_out, grad_tokens, grad_values)


def solution(mesh):
    return jax.shard_map(
        body,
        mesh=mesh,
        in_specs=(
            P(("dp", "mem"), None),
            P(),
            P(None, "dp"),
            P(("dp", "mem"), None),
            P(("dp", "mem"), None),
            P(("dp", "mem"), None),
            P(("dp", "mem"), None),
        ),
        out_specs=(P(("dp", "mem"), None), P(("dp", "mem"), None), P(("dp", "mem"), None)),
        check_vma=False,
    )
```

profile of v0, /device:TPU:0, one launch (start us, length us, event | category | flops | bytes accessed | tf_op | source)
XLA Modules:
  0.0 333.5 jit_solution(7504872009149720619)
XLA Ops:
  7.2 0.0 copy-start.1
  7.2 0.0 all-gather.2.cloned.1.call-start
  7.2 0.7 all-gather.2.cloned.1.call-update
  7.9 0.8 copy.18
  8.7 0.1 reshape.189
  8.8 0.1 reshape.191
  9.0 0.1 reshape.190
  9.1 0.6 reduce-window.6
  9.7 0.2 slice_reduce_fusion.1
  10.0 0.1 fusion.29
  10.1 1.4 scatter_custom_fusion
  11.6 3.5 %gather_fusion = s32[512]{0:T(512)S(1)} fusion(s32[257]{0:T(512)S(1)} %pad_add_fusion, s32[1024]{0:T(1024)S(1)} %pad_clamp_fusion.1), kind=kCustom, calls=%fused_computation | custom fusion | bytes 6144 | tf_op jit(solution)/shard_map/gather | solution.py:90
  15.1 0.7 all_to_all.12
  15.7 7.3 %all-to-all-start = ((s32[32,1,16]{2,1,0:T(1,128)}), s32[32,1,16]{2,1,0:T(1,128)S(1)}, u32[]{:S(2)}, u32[]{:S(2)}) async-start(s32[32,1,16]{2,1,0:T(1,128)} %bitcast.3), calls=%async_computation | async-start | bytes 32768 | tf_op jit(solution)/shard_map/all_to_all | solution.py:93
  23.0 0.0 copy-done.1
  23.1 1.0 mul.104
  24.1 0.0 copy-start.3
  24.1 0.0 copy-start
  24.1 2.4 mul.105
  26.6 0.0 copy-done.3
  26.6 0.0 copy-start.2
  26.6 0.1 copy.17
  26.7 0.1 mul.102
  26.8 0.0 copy-done
  26.8 0.2 fusion.24
  27.0 2.7 multiply_convert_fusion
  29.8 41.0 %all-gather.2.cloned.1.call-done = bf16[2048,2048]{1,0:T(8,128)(2,1)} async-done(((bf16[2048,512]{1,0:T(8,128)(2,1)}), bf16[2048,2048]{1,0:T(8,128)(2,1)}) %all-gather.2.cloned.1.call-update) | async-done | bytes 8388624 | tf_op jit(solution)/shard_map/all_gather | solution.py:63
  70.8 0.0 copy-done.2
  70.8 4.7 %convolution_convert_fusion.2 = bf16[128,2048]{1,0:T(8,128)(2,1)S(1)} fusion(bf16[2048,2048]{1,0:T(8,128)(2,1)} %all-gather.2.cloned.1.call-done, bf16[128,2048]{1,0:T(8,128)(2,1)S(1)} %copy-done, f32[2048]{0:T(1024)S(1)} %copy-done.2, f32[128]{0:T(128)S(1)} %add_rsqrt_fusion), kind=kOutput, calls=%fused_computation.14 | convolution fusion | flops 1075052544 | bytes 9445888 | tf_op jit(solution)/shard_map/dot_general | solution.py:68
  75.5 0.6 broadcast_in_dim.12
  76.1 1.2 concatenate.16
  77.3 1.7 fusion.2
  79.1 4.4 %gather_fusion.1 = bf16[512,4096]{1,0:T(8,128)(2,1)} fusion(bf16[257,4096]{1,0:T(8,128)(2,1)S(1)} %fusion.2, s32[1024]{0:T(1024)S(1)} %pad_clamp_fusion.1), kind=kCustom, calls=%fused_computation.1 | custom fusion | bytes 8390656 | tf_op jit(solution)/shard_map/gather | solution.py:88
  83.4 0.0 all-to-all-done
  83.4 4.9 %all-to-all-start.1 = ((bf16[32,16,4096]{2,1,0:T(8,128)(2,1)}), bf16[32,16,4096]{2,1,0:T(8,128)(2,1)}, u32[]{:S(2)}, u32[]{:S(2)}) async-start(bf16[32,16,4096]{2,1,0:T(8,128)(2,1)} %bitcast.31), calls=%async_computation.1 | async-start | bytes 8388608 | tf_op jit(solution)/shard_map/all_to_all | solution.py:92
  88.4 0.5 broadcast.281
  88.9 0.7 reduce.6
  89.6 0.1 eq.44
  89.7 94.5 %all-to-all-done.1 = bf16[32,16,4096]{2,1,0:T(8,128)(2,1)} async-done(((bf16[32,16,4096]{2,1,0:T(8,128)(2,1)}), bf16[32,16,4096]{2,1,0:T(8,128)(2,1)}, u32[]{:S(2)}, u32[]{:S(2)}) %all-to-all-start.1) | async-done | bytes 4194336 | tf_op jit(solution)/shard_map/all_to_all | solution.py:92
  184.1 0.0 copy-start.4
  184.1 5.6 %add_divide_fusion = f32[512,1024]{1,0:T(8,128)S(1)} fusion(bf16[1024,2048]{1,0:T(8,128)(2,1)} %param.10, bf16[512,4096]{1,0:T(8,128)(2,1)} %bitcast.5), kind=kOutput, calls=%fused_computation.19 | convolution fusion | flops 2149580800 | bytes 8388608 | tf_op jit(solution)/shard_map/dot_general | solution.py:10
  189.7 0.0 copy-done.4
  189.7 4.2 %fusion.4 = bf16[512,1024]{1,0:T(8,128)(2,1)S(1)} fusion(f32[512,1024]{1,0:T(8,128)S(1)} %add_divide_fusion, bf16[1024,2048]{1,0:T(8,128)(2,1)S(1)} %copy-done.4, bf16[512,4096]{1,0:T(8,128)(2,1)} %bitcast.5, s32[1024]{0:T(1024)S(1)} %add_select_fusion, s32[512]{0:T(512)S(1)} %eq.44), kind=kOutput, calls=%fused_computation.17 | convolution fusion | flops 2151153664 | bytes 9443328 | tf_op jit(solution)/shard_map/dot_general | solution.py:10
  193.9 0.0 copy-start.5
  193.9 2.4 convolution_convert_fusion.1
  196.4 0.0 copy-done.5
  196.4 2.4 convolution_convert_fusion
  198.8 2.4 pad_maximum_fusion
  201.2 3.8 %all-to-all-start.2 = ((bf16[32,16,4096]{2,1,0:T(8,128)(2,1)}), bf16[32,16,4096]{2,1,0:T(8,128)(2,1)}, u32[]{:S(2)}, u32[]{:S(2)}) async-start(bf16[32,16,4096]{2,1,0:T(8,128)(2,1)} %bitcast.32), calls=%async_computation.2 | async-start | bytes 8388608 | tf_op jit(solution)/shard_map/all_to_all | solution.py:96
  205.0 0.0 copy-start.6
  205.0 4.2 %fusion.5 = f32[1024,2048]{1,0:T(8,128)S(1)} fusion(bf16[512,4096]{1,0:T(8,128)(2,1)} %bitcast.5, f32[512,1024]{1,0:T(8,128)S(1)} %add_divide_fusion, s32[1024]{0:T(1024)S(1)} %add_select_fusion, s32[512]{0:T(512)S(1)} %eq.44), kind=kOutput, calls=%fused_computation.21 | convolution fusion | flops 2148532224 | bytes 12589056 | tf_op jit(solution)/shard_map/dot_general | solution.py:16
  209.2 0.0 copy-done.6
  209.2 6.3 %add_convert_fusion = bf16[1024,2048]{1,0:T(8,128)(2,1)} fusion(f32[1024,2048]{1,0:T(8,128)S(1)} %fusion.5, bf16[512,1024]{1,0:T(8,128)(2,1)S(1)} %copy-done.6, bf16[512,4096]{1,0:T(8,128)(2,1)} %bitcast.5), kind=kOutput, calls=%fused_computation.4 | convolution fusion | flops 2151677952 | bytes 15728640 | tf_op jit(solution)/shard_map/dot_general | solution.py:16
  215.5 85.3 %all-to-all-done.2 = bf16[32,16,4096]{2,1,0:T(8,128)(2,1)} async-done(((bf16[32,16,4096]{2,1,0:T(8,128)(2,1)}), bf16[32,16,4096]{2,1,0:T(8,128)(2,1)}, u32[]{:S(2)}, u32[]{:S(2)}) %all-to-all-start.2) | async-done | bytes 4194336 | tf_op jit(solution)/shard_map/all_to_all | solution.py:96
  300.7 6.6 %gather_fusion.2 = bf16[256,4096]{1,0:T(8,128)(2,1)S(1)} fusion(bf16[512,4096]{1,0:T(8,128)(2,1)} %bitcast.7, s32[1024]{0:T(1024)S(1)} %pad_clamp_fusion), kind=kCustom, calls=%fused_computation.2 | custom fusion | bytes 4195328 | tf_op jit(solution)/shard_map/gather | solution.py:105
  307.4 2.7 reshape.197
  310.1 4.2 %slice_reduce_fusion = bf16[128,2048]{1,0:T(8,128)(2,1)S(1)} fusion(bf16[128,2,4096]{2,1,0:T(2,128)(2,1)} %reshape.197), kind=kLoop, calls=%fused_computation.40 | loop fusion | flops 262144 | bytes 1572864 | tf_op jit(solution)/shard_map/reduce_sum | solution.py:111
  314.2 4.4 %multiply_reduce_fusion = f32[128,2048]{1,0:T(8,128)S(1)} fusion(bf16[128,2,4096]{2,1,0:T(2,128)(2,1)} %reshape.197, f32[128,2]{1,0:T(8,128)S(1)} %copy.17), kind=kLoop, calls=%fused_computation.18 | loop fusion | flops 1310720 | bytes 2098176 | tf_op jit(solution)/shard_map/reduce_sum | solution.py:110
  318.6 6.4 %fusion.20 = (f32[128]{0:T(128)S(1)}, f32[128,2048]{1,0:T(8,128)S(1)}) fusion(bf16[128,2048]{1,0:T(8,128)(2,1)S(1)} %copy-done, f32[128]{0:T(128)S(1)} %add_rsqrt_fusion, f32[2048]{0:T(1024)S(1)} %copy-done.2, bf16[128,2048]{1,0:T(8,128)(2,1)S(1)} %slice_reduce_fusion, bf16[2048,2048]{1,0:T(8,128)(2,1)} %all-gather.2.cloned.1.call-done), kind=kOutput, calls=%fused_computation.35 | convolution fusion | flops 1075052416 | bytes 10494976 | tf_op jit(solution)/shard_map/dot_general | solution.py:10
  324.9 1.7 fusion.23
  (14 shorter events, 0.1 us)
Async XLA Ops:
  7.2 15.9 %copy-start.1 = (bf16[128,2048]{1,0:T(8,128)(2,1)S(1)}, bf16[128,2048]{1,0:T(8,128)(2,1)}, u32[]{:S(2)}) copy-start(bf16[128,2048]{1,0:T(8,128)(2,1)} %param.13) | copy-start | bytes 1572868
  7.2 63.6 %all-gather.2.cloned.1.call-start = ((), (), s32[]{:S(2)}) async-start(), calls=%async_computation.3 | async-start | bytes 10485760 | tf_op jit(solution)/shard_map/all_gather | solution.py:63
  15.7 67.7 %all-to-all-start = ((s32[32,1,16]{2,1,0:T(1,128)}), s32[32,1,16]{2,1,0:T(1,128)S(1)}, u32[]{:S(2)}, u32[]{:S(2)}) async-start(s32[32,1,16]{2,1,0:T(1,128)} %bitcast.3), calls=%async_computation | async-start | bytes 32768 | tf_op jit(solution)/shard_map/all_to_all | solution.py:93
  24.1 2.5 copy-start.3
  24.1 2.7 copy-start
  26.6 44.2 %copy-start.2 = (f32[2048]{0:T(1024)S(1)}, f32[2048]{0:T(1024)}, u32[]{:S(2)}) copy-start(f32[2048]{0:T(1024)} %param.8) | copy-start | bytes 24580
  83.4 100.7 %all-to-all-start.1 = ((bf16[32,16,4096]{2,1,0:T(8,128)(2,1)}), bf16[32,16,4096]{2,1,0:T(8,128)(2,1)}, u32[]{:S(2)}, u32[]{:S(2)}) async-start(bf16[32,16,4096]{2,1,0:T(8,128)(2,1)} %bitcast.31), calls=%async_computation.1 | async-start | bytes 8388608 | tf_op jit(solution)/shard_map/all_to_all | solution.py:92
  184.1 5.6 %copy-start.4 = (bf16[1024,2048]{1,0:T(8,128)(2,1)S(1)}, bf16[1024,2048]{1,0:T(8,128)(2,1)}, u32[]{:S(2)}) copy-start(bf16[1024,2048]{1,0:T(8,128)(2,1)} %param.10) | copy-start | bytes 12582916
  193.9 2.5 copy-start.5
  201.2 99.6 %all-to-all-start.2 = ((bf16[32,16,4096]{2,1,0:T(8,128)(2,1)}), bf16[32,16,4096]{2,1,0:T(8,128)(2,1)}, u32[]{:S(2)}, u32[]{:S(2)}) async-start(bf16[32,16,4096]{2,1,0:T(8,128)(2,1)} %bitcast.32), calls=%async_computation.2 | async-start | bytes 8388608 | tf_op jit(solution)/shard_map/all_to_all | solution.py:96
  205.0 4.2 %copy-start.6 = (bf16[512,1024]{1,0:T(8,128)(2,1)S(1)}, bf16[512,1024]{1,0:T(8,128)(2,1)}, u32[]{:S(2)}) copy-start(bf16[512,1024]{1,0:T(8,128)(2,1)} %copy-done.5) | copy-start | bytes 3145732
Sparse Core Ops, SparseCore 0:
  9.6 61.1 all-gather.1
where the time goes:
time: 334 us
  waiting for transfers between devices  221 us (66%)
  matrix products  36 us (11%)
  local copies, waits for them, and re-layouts  26.9 us (8%)
  other arithmetic  18.8 us (6%)
  starting transfers between devices  16 us (5%)
  between operations  14.3 us (4%)
    all_to_all x1, waiting for transfers between devices, body(): lax.all_to_all(payload, ('dp', 'mem'), split_axis=0, concat_axis=0, tiled...  94.5 us
    all_to_all x1, waiting for transfers between devices, body(): lax.all_to_all(answer, ('dp', 'mem'), split_axis=0, concat_axis=0, tiled=...  85.3 us
    all_gather x1, waiting for transfers between devices, body(): weight_full = lax.all_gather(query_weight, 'dp', axis=1, tiled=True)  41 us
    dot_general x3, matrix products, against_rows(): lax.dot_general(left, table, (((1,), (1,)), ((), ())), preferred_element_...  16.1 us
    dot_general x2, matrix products, over_slots(): lax.dot_general(left, right, (((0,), (0,)), ((), ())), preferred_element_...  10.4 us
    all_to_all x1, starting transfers between devices, body(): lax.all_to_all(slot_ids, ('dp', 'mem'), split_axis=0, concat_axis=0, tile...  7.3 us
  transfers between devices with their start and end apart: 4, of which 3 were waited for; matrix products, arithmetic and copies ran while one was open for 11% of the time, Pallas kernels for 0%

commit v1 on v0

v1 whole, which is shorter than its diff:
```python
import jax
import jax.numpy as jnp
from jax import lax
from jax.sharding import PartitionSpec as P

BLOCK = 64
AXES = ("dp", "mem")
BF = jnp.bfloat16
F32 = jnp.float32


def dot(left, right, left_dim=1, right_dim=0):
    return lax.dot_general(
        left, right, (((left_dim,), (right_dim,)), ((), ())), preferred_element_type=F32
    )


def exchange(rows, owner_count):
    slots, features = rows.shape
    out = lax.all_to_all(
        rows.reshape(owner_count, slots // owner_count, features),
        AXES,
        split_axis=0,
        concat_axis=0,
        tiled=True,
    )
    return out.reshape(slots, features)


def body(tokens, norm_gain, query_weight, values, blocks, weights, out_cotangent):
    token_count, features = tokens.shape
    top_count = blocks.shape[1]
    value_rows = values.shape[0]
    span_blocks = value_rows // BLOCK
    owner_count = lax.axis_size("dp") * lax.axis_size("mem")
    pair_count = token_count * top_count
    capacity = 2 * pair_count // owner_count
    slot_total = owner_count * capacity
    score_scale = float(features) ** (-0.5)
    me = lax.axis_index(AXES)

    all_blocks = lax.all_gather(blocks, AXES, axis=0, tiled=True)
    weight_full = lax.all_gather(query_weight, "dp", axis=1, tiled=True)

    earlier = (
        jnp.arange(pair_count)[:, None] > jnp.arange(pair_count)[None, :]
    ).astype(BF)

    flat_ids = blocks.reshape(pair_count)
    owner_of = flat_ids // span_blocks
    hits = owner_of[:, None] == jnp.arange(owner_count, dtype=jnp.int32)[None, :]
    ranks = dot(earlier, hits.astype(BF))
    slot_of = jnp.sum(jnp.where(hits, ranks, 0.0), axis=1).astype(jnp.int32)
    target = (owner_of * capacity + slot_of).reshape(token_count, top_count)
    slot_ids = jnp.arange(slot_total, dtype=jnp.int32)
    picks = [(target[:, k][None, :] == slot_ids[:, None]) for k in range(top_count)]
    pick_rows = sum(p.astype(BF) for p in picks)
    slot_weight = sum(
        jnp.sum(jnp.where(p, weights[:, k][None, :], 0.0), axis=1, keepdims=True)
        for k, p in enumerate(picks)
    )

    cot_load = (slot_weight * dot(pick_rows, out_cotangent)).astype(BF)
    cot_rows = exchange(cot_load, owner_count)

    exact_tokens = tokens.astype(F32)
    rms_rows = lax.rsqrt(jnp.mean(exact_tokens * exact_tokens, axis=1, keepdims=True) + 1e-06)
    unit_rows = exact_tokens * rms_rows
    normed = (unit_rows * norm_gain).astype(BF)
    normed_rows = exchange(dot(pick_rows, normed).astype(BF), owner_count)

    their_ids = all_blocks.reshape(owner_count, pair_count)
    mine = their_ids // span_blocks == me
    their_rank = dot(mine.astype(BF), earlier, 1, 1).astype(jnp.int32)
    rank_here = jnp.where(mine, their_rank, -1)
    local_next = (their_ids % span_blocks + 1)[:, None, :]
    at_slot = rank_here[:, None, :] == jnp.arange(capacity, dtype=jnp.int32)[None, :, None]
    block_here = jnp.sum(jnp.where(at_slot, local_next, 0), axis=2) - 1
    row_block = jnp.arange(value_rows, dtype=jnp.int32) // BLOCK
    in_block = block_here.reshape(slot_total)[:, None] == row_block[None, :]

    cot_scores = dot(cot_rows, values, 1, 1)
    query_rows = dot(normed_rows, weight_full).astype(BF)
    scores = dot(query_rows, values, 1, 1) * score_scale
    sigmoid_of = jax.nn.sigmoid(scores)
    gate_values = jnp.where(in_block, sigmoid_of, 0.0).astype(BF)
    parts_back = exchange(dot(gate_values, values).astype(BF), owner_count)
    score_grads = jnp.where(
        in_block, cot_scores * sigmoid_of * (1.0 - sigmoid_of) * score_scale, 0.0
    ).astype(BF)
    grads_back = exchange(dot(score_grads, values).astype(BF), owner_count)
    grad_values = (dot(gate_values, cot_rows, 0, 0) + dot(score_grads, query_rows, 0, 0)).astype(BF)

    mixed = sum(
        weights[:, k][:, None] * dot(p.astype(BF), parts_back, 0, 0) for k, p in enumerate(picks)
    )
    layer_out = exact_tokens + mixed
    query_grad = dot(pick_rows, grads_back, 0, 0).astype(BF)
    unit_grad = dot(query_grad, weight_full, 1, 1) * norm_gain
    grad_tokens = out_cotangent.astype(F32) + rms_rows * (
        unit_grad - unit_rows * jnp.mean(unit_grad * unit_rows, axis=1, keepdims=True)
    )
    return (layer_out, grad_tokens, grad_values)


def solution(mesh):
    rows = P(AXES, None)
    return jax.shard_map(
        body,
        mesh=mesh,
        in_specs=(rows, P(), P(None, "dp"), rows, rows, rows, rows),
        out_specs=(rows, rows, rows),
        check_vma=False,
    )
```

time: 334 us -> 320 us (0.958)
  blocking collectives: 0 us -> 104 us
  waiting for transfers between devices: 221 us -> 124 us
  local copies, waits for them, and re-layouts: 26.9 us -> 6.67 us
  other arithmetic: 18.8 us -> 2.51 us
  matrix products: 36 us -> 52 us
    all_gather x0 -> x1, blocking collectives: none -> 104 us  [body(): all_blocks = lax.all_gather(blocks, AXES, axis=0, tiled=True)]
    all_to_all x3 -> x4, waiting for transfers between devices: 180 us -> 123 us  [exchange(): lax.all_to_all(rows.reshape(owner_count, slots // owner_count, features),...]
    all_gather x1, waiting for transfers between devices: 41 us -> 0.01 us  [body(): weight_full = lax.all_gather(query_weight, 'dp', axis=1, tiled=True)]
    dot_general x8 -> x14, matrix products: 36 us -> 52 us  [dot(): lax.dot_general(left, right, (((left_dim,), (right_dim,)), ((), ())), pre...]
    gather x3 -> x0, local copies, waits for them, and re-layouts: 14.5 us -> none  [the longest x1 6.61 us: body(): returned.reshape(slot_total, 2 * features)[target]]
    reduce_sum x3 -> x2, other arithmetic: 8.61 us -> 0.86 us  [the longest x1 0.64 us: body(): block_here = jnp.sum(jnp.where(at_slot, local_next, 0), axis=2) - 1]
    concatenate x3 -> x0, other arithmetic: 4.16 us -> none  [the longest x1 2.42 us: serve_lookups(): jnp.concatenate([block_parts, query_parts], axis=1)]
    mul x3 -> x1, local copies, waits for them, and re-layouts: 3.62 us -> 0.01 us  [body(): weights[:, k][:, None] * dot(p.astype(BF), parts_back, 0, 0)]
  transfers between devices with their start and end apart: 4 -> 5, of which waited for: 3 -> 3; matrix products, arithmetic and copies ran while one was open for 11% -> 14% of each run, Pallas kernels for 0% -> 0%
where the time goes in v1:
time: 320 us
  waiting for transfers between devices  124 us (39%)
  blocking collectives  104 us (32%)
  matrix products  52 us (16%)
  starting transfers between devices  16.5 us (5%)
  between operations  14.4 us (4%)
  local copies, waits for them, and re-layouts  6.67 us (2%)
    all_to_all x4, waiting for transfers between devices, exchange(): lax.all_to_all(rows.reshape(owner_count, slots // owner_count, features),...  123 us
    all_gather x1, blocking collectives, body(): all_blocks = lax.all_gather(blocks, AXES, axis=0, tiled=True)  104 us
    dot_general x14, matrix products, dot(): lax.dot_general(left, right, (((left_dim,), (right_dim,)), ((), ())), pre...  52 us
    all_to_all x4, starting transfers between devices, exchange(): lax.all_to_all(rows.reshape(owner_count, slots // owner_count, features),...  16.5 us
  transfers between devices with their start and end apart: 5, of which 3 were waited for; matrix products, arithmetic and copies ran while one was open for 14% of the time, Pallas kernels for 0%

profile of v1, /device:TPU:0, one launch (start us, length us, event | category | flops | bytes accessed | tf_op | source)
XLA Modules:
  0.0 319.8 jit_solution(10964201249753276279)
XLA Ops:
  7.2 0.0 copy-start.7
  7.2 0.0 copy-start
  7.2 0.0 copy-start.6
  7.2 0.0 all-gather.2.cloned.1.call-start
  7.2 0.7 all-gather.2.cloned.1.call-update
  7.9 0.0 copy-done.7
  7.9 0.1 copy.29
  8.1 0.1 copy.34
  8.2 0.1 reshape.133
  8.4 0.2 fusion.8
  8.6 0.1 convert_element_type.59
  8.7 0.1 fusion.37
  8.8 0.2 slice_reduce_fusion.1
  9.0 0.0 copy-done
  9.0 0.2 fusion.14
  9.2 0.0 copy-done.6
  9.2 2.1 convolution_convert_fusion.2
  11.3 7.3 %all-to-all-start = ((bf16[32,16,2048]{2,1,0:T(8,128)(2,1)}), bf16[32,16,2048]{2,1,0:T(8,128)(2,1)S(1)}, u32[]{:S(2)}, u32[]{:S(2)}) async-start(bf16[32,16,2048]{2,1,0:T(8,128)(2,1)} %bitcast.1), calls=%async_computation | async-start | bytes 4194304 | tf_op jit(solution)/shard_map/all_to_all | solution.py:20
  18.6 0.0 copy-done.8
  18.6 0.2 select_reduce_fusion.1
  18.9 0.0 copy-done.5
  18.9 2.0 multiply_convert_fusion
  20.9 47.8 %all-to-all-done = bf16[32,16,2048]{2,1,0:T(8,128)(2,1)S(1)} async-done(((bf16[32,16,2048]{2,1,0:T(8,128)(2,1)}), bf16[32,16,2048]{2,1,0:T(8,128)(2,1)S(1)}, u32[]{:S(2)}, u32[]{:S(2)}) %all-to-all-start) | async-done | bytes 2097184 | tf_op jit(solution)/shard_map/all_to_all | solution.py:20
  68.7 1.3 copy-done.3
  70.0 3.5 %all-to-all-start.2 = ((bf16[32,16,2048]{2,1,0:T(8,128)(2,1)}), bf16[32,16,2048]{2,1,0:T(8,128)(2,1)}, u32[]{:S(2)}, u32[]{:S(2)}) async-start(bf16[32,16,2048]{2,1,0:T(8,128)(2,1)} %bitcast.6), calls=%async_computation.2 | async-start | bytes 4194304 | tf_op jit(solution)/shard_map/all_to_all | solution.py:20
  73.5 103.7 %all_gather.6 = s32[4096,2]{0,1:T(2,128)S(1)} all-gather(s32[128,2]{0,1:T(2,128)S(1)} %copy-done.7), channel_id=1, replica_groups=mesh['dp'=4,'mem'=8] {'dp','mem'}, dimensions={0}, use_global_device_ids=true | all-gather | bytes 33792 | tf_op jit(solution)/shard_map/all_gather | solution.py:42
  177.2 0.6 copy.37
  177.9 1.2 reshape.134
  179.1 0.2 fusion.7
  179.3 0.6 select_reduce_fusion
  180.0 0.1 sub.36
  180.1 0.0 all-gather.2.cloned.1.call-done
  180.1 0.0 copy-start.9
  180.1 8.7 %convolution_convert_fusion.3 = bf16[512,2048]{1,0:T(8,128)(2,1)S(1)} fusion(bf16[512,2048]{1,0:T(8,128)(2,1)} %bitcast.32, bf16[2048,2048]{1,0:T(8,128)(2,1)} %all-gather.2.cloned.1.call-done), kind=kOutput, calls=%fused_computation.5 | convolution fusion | flops 4296015872 | bytes 12582912 | tf_op jit(solution)/shard_map/dot_general | solution.py:13
  188.7 0.0 copy-start.11
  188.8 1.3 copy-done.11
  190.1 0.0 copy-done.9
  190.1 2.6 add_divide_fusion
  192.7 0.0 copy-start.4
  192.7 0.0 all-to-all-done.2
  192.7 0.0 copy-start.10
  192.7 6.2 %fusion.3 = bf16[512,1024]{1,0:T(8,128)(2,1)S(1)} fusion(f32[512,1024]{1,0:T(8,128)S(1)} %add_divide_fusion, bf16[512,2048]{1,0:T(8,128)(2,1)} %bitcast.7, bf16[1024,2048]{1,0:T(8,128)(2,1)} %param.10, s32[1024]{0:T(1024)S(1)} %add_select_fusion.3, s32[512]{0:T(512)S(1)} %sub.36), kind=kOutput, calls=%fused_computation.15 | convolution fusion | flops 2151153664 | bytes 9443328 | tf_op jit(solution)/shard_map/dot_general | solution.py:13
  198.9 0.0 copy-done.4
  198.9 0.0 copy-done.10
  198.9 0.0 copy-start.13
  198.9 3.7 %convolution_convert_fusion = bf16[512,2048]{1,0:T(8,128)(2,1)} fusion(bf16[512,1024]{1,0:T(8,128)(2,1)S(1)} %fusion.3, bf16[1024,2048]{1,0:T(8,128)(2,1)S(1)} %copy-done.10), kind=kOutput, calls=%fused_computation.2 | convolution fusion | flops 2148532224 | bytes 7340032 | tf_op jit(solution)/shard_map/dot_general | solution.py:13
  202.6 0.0 copy-done.13
  202.6 2.9 all-to-all-start.3
  205.6 6.5 %convolution_convert_fusion.1 = bf16[512,2048]{1,0:T(8,128)(2,1)} fusion(bf16[1024,2048]{1,0:T(8,128)(2,1)} %param.10, f32[512,1024]{1,0:T(8,128)} %copy-done.4, s32[1024]{0:T(1024)S(1)} %add_select_fusion.3, s32[512]{0:T(512)S(1)} %sub.36), kind=kOutput, calls=%fused_computation.3 | convolution fusion | flops 2149580800 | bytes 8394752 | tf_op jit(solution)/shard_map/dot_general | solution.py:13
  212.1 43.3 %all-to-all-done.3 = bf16[32,16,2048]{2,1,0:T(8,128)(2,1)S(1)} async-done(((bf16[32,16,2048]{2,1,0:T(8,128)(2,1)}), bf16[32,16,2048]{2,1,0:T(8,128)(2,1)S(1)}, u32[]{:S(2)}, u32[]{:S(2)}) %all-to-all-start.3) | async-done | bytes 2097184 | tf_op jit(solution)/shard_map/all_to_all | solution.py:20
  255.5 1.3 copy-done.1
  256.8 2.7 all-to-all-start.1
  259.5 0.0 copy-start.12
  259.5 0.0 copy-start.14
  259.5 4.9 %fusion.61 = f32[1024,2048]{1,0:T(8,128)S(1)} fusion(bf16[512,2048]{1,0:T(8,128)(2,1)} %bitcast.7, f32[512,1024]{1,0:T(8,128)} %copy-done.4, s32[1024]{0:T(1024)S(1)} %add_select_fusion.3, s32[512]{0:T(512)S(1)} %sub.36), kind=kOutput, calls=%fused_computation.104 | convolution fusion | flops 2148532224 | bytes 12589056 | tf_op jit(solution)/shard_map/dot_general | solution.py:13
  264.4 0.0 copy-done.12
  264.4 4.7 %add_convert_fusion = bf16[1024,2048]{1,0:T(8,128)(2,1)} fusion(f32[1024,2048]{1,0:T(8,128)S(1)} %fusion.61, bf16[512,1024]{1,0:T(8,128)(2,1)S(1)} %copy-done.14, bf16[512,2048]{1,0:T(8,128)(2,1)S(1)} %copy-done.12), kind=kOutput, calls=%fused_computation | convolution fusion | flops 2151677952 | bytes 15728640 | tf_op jit(solution)/shard_map/dot_general | solution.py:13
  269.1 8.3 %fusion.10 = (f32[128]{0:T(128)S(1)}, f32[128,2048]{1,0:T(8,128)}) fusion(bf16[128,2048]{1,0:T(8,128)(2,1)S(1)} %copy-done, f32[128]{0:T(128)S(1)} %add_rsqrt_fusion, f32[2048]{0:T(1024)S(1)} %copy-done.6, bf16[2048,2048]{1,0:T(8,128)(2,1)} %all-gather.2.cloned.1.call-done, bf16[512,2048]{1,0:T(8,128)(2,1)} %bitcast.31, s32[128]{0:T(128)S(1)} %get-tuple-element.4, ...), kind=kOutput, calls=%fused_computation.27 | convolution fusion | flops 1344274304 | bytes 12068864 | tf_op jit(solution)/shard_map/dot_general | solution.py:13
  277.4 32.2 %all-to-all-done.1 = bf16[32,16,2048]{2,1,0:T(8,128)(2,1)S(1)} async-done(((bf16[32,16,2048]{2,1,0:T(8,128)(2,1)}), bf16[32,16,2048]{2,1,0:T(8,128)(2,1)S(1)}, u32[]{:S(2)}, u32[]{:S(2)}) %all-to-all-start.1) | async-done | bytes 2097184 | tf_op jit(solution)/shard_map/all_to_all | solution.py:20
  309.6 0.5 convolution_multiply_fusion.2
  310.1 0.0 copy-start.2
  310.1 1.5 fusion.1
  311.6 0.0 copy-done.2
  311.6 1.3 fusion.13
  (15 shorter events, 0.1 us)
Async XLA Ops:
  7.2 0.8 copy-start.7
  7.2 1.8 copy-start
  7.2 2.0 copy-start.6
  7.2 172.9 %all-gather.2.cloned.1.call-start = ((), (), s32[]{:S(2)}) async-start(), calls=%async_computation.4 | async-start | bytes 10485760 | tf_op jit(solution)/shard_map/all_gather | solution.py:43
  11.3 7.3 %copy-start.8 = (f32[128,2]{0,1:T(2,128)S(1)}, f32[128,2]{0,1:T(2,128)}, u32[]{:S(2)}) copy-start(f32[128,2]{0,1:T(2,128)} %param.12) | copy-start | bytes 3076
  11.3 7.6 %copy-start.5 = (bf16[128,2048]{1,0:T(8,128)(2,1)S(1)}, bf16[128,2048]{1,0:T(8,128)(2,1)}, u32[]{:S(2)}) copy-start(bf16[128,2048]{1,0:T(8,128)(2,1)} %param.13) | copy-start | bytes 1572868
  11.3 57.4 %all-to-all-start = ((bf16[32,16,2048]{2,1,0:T(8,128)(2,1)}), bf16[32,16,2048]{2,1,0:T(8,128)(2,1)S(1)}, u32[]{:S(2)}, u32[]{:S(2)}) async-start(bf16[32,16,2048]{2,1,0:T(8,128)(2,1)} %bitcast.1), calls=%async_computation | async-start | bytes 4194304 | tf_op jit(solution)/shard_map/all_to_all | solution.py:20
  68.7 1.3 copy-start.3
  70.0 122.7 %all-to-all-start.2 = ((bf16[32,16,2048]{2,1,0:T(8,128)(2,1)}), bf16[32,16,2048]{2,1,0:T(8,128)(2,1)}, u32[]{:S(2)}, u32[]{:S(2)}) async-start(bf16[32,16,2048]{2,1,0:T(8,128)(2,1)} %bitcast.6), calls=%async_computation.2 | async-start | bytes 4194304 | tf_op jit(solution)/shard_map/all_to_all | solution.py:20
  180.1 10.0 %copy-start.9 = (bf16[1024,2048]{1,0:T(8,128)(2,1)S(1)}, bf16[1024,2048]{1,0:T(8,128)(2,1)}, u32[]{:S(2)}) copy-start(bf16[1024,2048]{1,0:T(8,128)(2,1)} %param.10) | copy-start | bytes 12582916
  188.7 1.3 copy-start.11
  192.7 6.2 %copy-start.4 = (f32[512,1024]{1,0:T(8,128)}, f32[512,1024]{1,0:T(8,128)S(1)}, u32[]{:S(2)}) copy-start(f32[512,1024]{1,0:T(8,128)S(1)} %add_divide_fusion) | copy-start | bytes 6291460
  192.7 6.2 %copy-start.10 = (bf16[1024,2048]{1,0:T(8,128)(2,1)S(1)}, bf16[1024,2048]{1,0:T(8,128)(2,1)}, u32[]{:S(2)}) copy-start(bf16[1024,2048]{1,0:T(8,128)(2,1)} %param.10) | copy-start | bytes 12582916
  198.9 3.7 %copy-start.13 = (bf16[512,1024]{1,0:T(8,128)(2,1)}, bf16[512,1024]{1,0:T(8,128)(2,1)S(1)}, u32[]{:S(2)}) copy-start(bf16[512,1024]{1,0:T(8,128)(2,1)S(1)} %fusion.3) | copy-start | bytes 3145732
  202.6 52.8 %all-to-all-start.3 = ((bf16[32,16,2048]{2,1,0:T(8,128)(2,1)}), bf16[32,16,2048]{2,1,0:T(8,128)(2,1)S(1)}, u32[]{:S(2)}, u32[]{:S(2)}) async-start(bf16[32,16,2048]{2,1,0:T(8,128)(2,1)} %bitcast.34), calls=%async_computation.3 | async-start | bytes 4194304 | tf_op jit(solution)/shard_map/all_to_all | solution.py:20
  255.5 1.3 copy-start.1
  256.8 52.8 %all-to-all-start.1 = ((bf16[32,16,2048]{2,1,0:T(8,128)(2,1)}), bf16[32,16,2048]{2,1,0:T(8,128)(2,1)S(1)}, u32[]{:S(2)}, u32[]{:S(2)}) async-start(bf16[32,16,2048]{2,1,0:T(8,128)(2,1)} %bitcast.33), calls=%async_computation.1 | async-start | bytes 4194304 | tf_op jit(solution)/shard_map/all_to_all | solution.py:20
  259.5 4.9 %copy-start.12 = (bf16[512,2048]{1,0:T(8,128)(2,1)S(1)}, bf16[512,2048]{1,0:T(8,128)(2,1)}, u32[]{:S(2)}) copy-start(bf16[512,2048]{1,0:T(8,128)(2,1)} %copy-done.11) | copy-start | bytes 6291460
  259.5 4.9 %copy-start.14 = (bf16[512,1024]{1,0:T(8,128)(2,1)S(1)}, bf16[512,1024]{1,0:T(8,128)(2,1)}, u32[]{:S(2)}) copy-start(bf16[512,1024]{1,0:T(8,128)(2,1)} %copy-done.13) | copy-start | bytes 3145732
  310.1 1.5 copy-start.2
Sparse Core Ops, SparseCore 0:
  9.6 99.5 all-gather.1

commit v2 on v1

--- a/solution.py
+++ b/solution.py
@@ -4,6 +4,7 @@
 from jax.sharding import PartitionSpec as P
 
 BLOCK = 64
+LANES = 128
 AXES = ("dp", "mem")
 BF = jnp.bfloat16
 F32 = jnp.float32
@@ -37,9 +38,6 @@
     capacity = 2 * pair_count // owner_count
     slot_total = owner_count * capacity
     score_scale = float(features) ** (-0.5)
-    me = lax.axis_index(AXES)
-
-    all_blocks = lax.all_gather(blocks, AXES, axis=0, tiled=True)
     weight_full = lax.all_gather(query_weight, "dp", axis=1, tiled=True)
 
     earlier = (
@@ -60,31 +58,40 @@
         for k, p in enumerate(picks)
     )
 
-    cot_load = (slot_weight * dot(pick_rows, out_cotangent)).astype(BF)
-    cot_rows = exchange(cot_load, owner_count)
+    local_next = blocks % span_blocks + 1
+    slot_block = sum(
+        jnp.sum(jnp.where(p, local_next[:, k][None, :], 0), axis=1, keepdims=True)
+        for k, p in enumerate(picks)
+    )
 
     exact_tokens = tokens.astype(F32)
     rms_rows = lax.rsqrt(jnp.mean(exact_tokens * exact_tokens, axis=1, keepdims=True) + 1e-06)
     unit_rows = exact_tokens * rms_rows
     normed = (unit_rows * norm_gain).astype(BF)
-    normed_rows = exchange(dot(pick_rows, normed).astype(BF), owner_count)
+    load = jnp.concatenate(
+        [
+            dot(pick_rows, normed).astype(BF),
+            jnp.broadcast_to(slot_block.astype(BF), (slot_total, LANES)),
+        ],
+        axis=1,
+    )
+    arrived = exchange(load, owner_count)
 
-    their_ids = all_blocks.reshape(owner_count, pair_count)
-    mine = their_ids // span_blocks == me
-    their_rank = dot(mine.astype(BF), earlier, 1, 1).astype(jnp.int32)
-    rank_here = jnp.where(mine, their_rank, -1)
-    local_next = (their_ids % span_blocks + 1)[:, None, :]
-    at_slot = rank_here[:, None, :] == jnp.arange(capacity, dtype=jnp.int32)[None, :, None]
-    block_here = jnp.sum(jnp.where(at_slot, local_next, 0), axis=2) - 1
+    cot_load = (slot_weight * dot(pick_rows, out_cotangent)).astype(BF)
+    cot_load, arrived = lax.optimization_barrier((cot_load, arrived))
+    cot_rows = exchange(cot_load, owner_count)
+
+    normed_rows = arrived[:, :features]
+    block_here = arrived[:, features : features + 1].astype(jnp.int32) - 1
     row_block = jnp.arange(value_rows, dtype=jnp.int32) // BLOCK
-    in_block = block_here.reshape(slot_total)[:, None] == row_block[None, :]
+    in_block = block_here == row_block[None, :]
 
-    cot_scores = dot(cot_rows, values, 1, 1)
     query_rows = dot(normed_rows, weight_full).astype(BF)
     scores = dot(query_rows, values, 1, 1) * score_scale
     sigmoid_of = jax.nn.sigmoid(scores)
     gate_values = jnp.where(in_block, sigmoid_of, 0.0).astype(BF)
     parts_back = exchange(dot(gate_values, values).astype(BF), owner_count)
+    cot_scores = dot(cot_rows, values, 1, 1)
     score_grads = jnp.where(
         in_block, cot_scores * sigmoid_of * (1.0 - sigmoid_of) * score_scale, 0.0
     ).astype(BF)

time: 320 us -> 257 us (0.80)
  blocking collectives: 104 us -> 0 us
  waiting for transfers between devices: 124 us -> 162 us
    all_gather x1 -> x0, blocking collectives: 104 us -> none  [body(): all_blocks = lax.all_gather(blocks, AXES, axis=0, tiled=True)]
    all_gather x1, waiting for transfers between devices: 0.01 us -> 33.2 us  [body(): weight_full = lax.all_gather(query_weight, 'dp', axis=1, tiled=True)]
    all_to_all x4, waiting for transfers between devices: 123 us -> 128 us  [exchange(): lax.all_to_all(rows.reshape(owner_count, slots // owner_count, features),...]
    dot_general x14 -> x13, matrix products: 52 us -> 51.8 us  [dot(): lax.dot_general(left, right, (((left_dim,), (right_dim,)), ((), ())), pre...]
  transfers between devices with their start and end apart: 5 -> 5, of which waited for: 3 -> 5; matrix products, arithmetic and copies ran while one was open for 14% -> 17% of each run, Pallas kernels for 0% -> 0%
where the time goes in v2:
time: 257 us; the launch traced here: 256 us
  waiting for transfers between devices  162 us (63%)
  matrix products  51.8 us (20%)
  starting transfers between devices  18.4 us (7%)
  between operations  14.3 us (6%)
  local copies, waits for them, and re-layouts  5.16 us (2%)
  other arithmetic  4.71 us (2%)
    all_to_all x4, waiting for transfers between devices, exchange(): lax.all_to_all(rows.reshape(owner_count, slots // owner_count, features),...  128 us
    dot_general x13, matrix products, dot(): lax.dot_general(left, right, (((left_dim,), (right_dim,)), ((), ())), pre...  51.8 us
    all_gather x1, waiting for transfers between devices, body(): weight_full = lax.all_gather(query_weight, 'dp', axis=1, tiled=True)  33.2 us
    all_to_all x4, starting transfers between devices, exchange(): lax.all_to_all(rows.reshape(owner_count, slots // owner_count, features),...  18.3 us
  transfers between devices with their start and end apart: 5, of which 5 were waited for; matrix products, arithmetic and copies ran while one was open for 17% of the time, Pallas kernels for 0%

profile of v2, /device:TPU:0, one launch (start us, length us, event | category | flops | bytes accessed | tf_op | source)
XLA Modules:
  0.0 256.2 jit_solution(122027495706196399)
XLA Ops:
  7.2 0.0 copy-start.7
  7.2 0.0 copy-start
  7.2 0.0 copy-start.6
  7.2 0.0 all-gather.2.cloned.1.call-start
  7.2 0.7 all-gather.2.cloned.1.call-update
  7.9 0.0 copy-done.7
  7.9 0.1 copy.27
  8.1 0.1 copy.32
  8.2 0.1 reshape.110
  8.4 0.2 fusion.8
  8.6 0.1 convert_element_type.66
  8.7 0.1 fusion.37
  8.8 0.2 slice_reduce_fusion
  9.0 0.2 slice_reduce_fusion.2
  9.2 0.2 select_reduce_fusion
  9.4 0.0 copy-done
  9.4 0.2 fusion.14
  9.6 0.0 copy-done.6
  9.6 0.8 convolution_convert_fusion.2
  10.4 0.1 broadcast_in_dim.81
  10.6 1.6 pad_maximum_fusion
  12.1 0.0 copy-start.5
  12.1 7.3 %all-to-all-start = ((bf16[32,16,2176]{2,1,0:T(8,128)(2,1)}), bf16[32,16,2176]{2,1,0:T(8,128)(2,1)S(1)}, u32[]{:S(2)}, u32[]{:S(2)}) async-start(bf16[32,16,2176]{2,1,0:T(8,128)(2,1)} %bitcast.2), calls=%async_computation | async-start | bytes 4456448 | tf_op jit(solution)/shard_map/all_to_all | solution.py:21
  19.4 0.0 copy-done.8
  19.4 0.2 select_reduce_fusion.2
  19.7 0.0 copy-done.5
  19.7 2.0 multiply_convert_fusion
  21.7 50.7 %all-to-all-done = bf16[32,16,2176]{2,1,0:T(8,128)(2,1)S(1)} async-done(((bf16[32,16,2176]{2,1,0:T(8,128)(2,1)}), bf16[32,16,2176]{2,1,0:T(8,128)(2,1)S(1)}, u32[]{:S(2)}, u32[]{:S(2)}) %all-to-all-start) | async-done | bytes 2228256 | tf_op jit(solution)/shard_map/all_to_all | solution.py:21
  72.4 0.0 copy-start.4
  72.4 1.4 copy-done.4
  73.8 2.9 %all-to-all-start.2 = ((bf16[32,16,2048]{2,1,0:T(8,128)(2,1)}), bf16[32,16,2048]{2,1,0:T(8,128)(2,1)S(1)}, u32[]{:S(2)}, u32[]{:S(2)}) async-start(bf16[32,16,2048]{2,1,0:T(8,128)(2,1)} %bitcast.6), calls=%async_computation.2 | async-start | bytes 4194304 | tf_op jit(solution)/shard_map/all_to_all | solution.py:21
  76.7 1.1 add_reduce_fusion
  77.8 33.2 %all-gather.2.cloned.1.call-done = bf16[2048,2048]{1,0:T(8,128)(2,1)} async-done(((bf16[2048,512]{1,0:T(8,128)(2,1)}), bf16[2048,2048]{1,0:T(8,128)(2,1)}) %all-gather.2.cloned.1.call-update) | async-done | bytes 8388624 | tf_op jit(solution)/shard_map/all_gather | solution.py:41
  111.0 0.0 copy-start.9
  111.0 8.7 %convolution_convert_fusion.3 = bf16[512,2048]{1,0:T(8,128)(2,1)S(1)} fusion(bf16[2048,2048]{1,0:T(8,128)(2,1)} %all-gather.2.cloned.1.call-done, bf16[512,2176]{1,0:T(8,128)(2,1)} %bitcast.34), kind=kOutput, calls=%fused_computation.5 | convolution fusion | flops 4296015872 | bytes 12582912 | tf_op jit(solution)/shard_map/dot_general | solution.py:14
  119.7 0.0 copy-start.11
  119.7 1.4 copy-done.11
  121.1 0.0 copy-done.9
  121.1 3.9 %add_divide_fusion = f32[512,1024]{1,0:T(8,128)} fusion(bf16[512,2048]{1,0:T(8,128)(2,1)S(1)} %convolution_convert_fusion.3, bf16[1024,2048]{1,0:T(8,128)(2,1)S(1)} %copy-done.9), kind=kOutput, calls=%fused_computation.17 | convolution fusion | flops 2149580800 | bytes 8388608 | tf_op jit(solution)/shard_map/dot_general | solution.py:14
  125.0 1.6 all-to-all-done.2
  126.6 6.2 %fusion.3 = bf16[512,1024]{1,0:T(8,128)(2,1)S(1)} fusion(f32[512,1024]{1,0:T(8,128)} %add_divide_fusion, bf16[512,2048]{1,0:T(8,128)(2,1)S(1)} %bitcast.30, bf16[1024,2048]{1,0:T(8,128)(2,1)} %param.10, s32[1024]{0:T(1024)S(1)} %add_select_fusion.2, s32[512]{0:T(512)S(1)} %add_reduce_fusion), kind=kOutput, calls=%fused_computation.16 | convolution fusion | flops 2151153664 | bytes 9443328 | tf_op jit(solution)/shard_map/dot_general | solution.py:14
  132.8 0.0 copy-done.1
  132.8 0.0 copy-done.10
  132.9 0.0 copy-start.13
  132.9 3.7 %convolution_convert_fusion = bf16[512,2048]{1,0:T(8,128)(2,1)} fusion(bf16[512,1024]{1,0:T(8,128)(2,1)S(1)} %fusion.3, bf16[1024,2048]{1,0:T(8,128)(2,1)S(1)} %copy-done.10), kind=kOutput, calls=%fused_computation.2 | convolution fusion | flops 2148532224 | bytes 7340032 | tf_op jit(solution)/shard_map/dot_general | solution.py:14
  136.6 0.0 copy-done.13
  136.6 5.2 %all-to-all-start.3 = ((bf16[32,16,2048]{2,1,0:T(8,128)(2,1)}), bf16[32,16,2048]{2,1,0:T(8,128)(2,1)S(1)}, u32[]{:S(2)}, u32[]{:S(2)}) async-start(bf16[32,16,2048]{2,1,0:T(8,128)(2,1)} %bitcast.36), calls=%async_computation.3 | async-start | bytes 4194304 | tf_op jit(solution)/shard_map/all_to_all | solution.py:21
  141.7 6.5 %convolution_convert_fusion.1 = bf16[512,2048]{1,0:T(8,128)(2,1)} fusion(bf16[1024,2048]{1,0:T(8,128)(2,1)} %param.10, f32[512,1024]{1,0:T(8,128)} %add_divide_fusion, s32[1024]{0:T(1024)S(1)} %add_select_fusion.2, s32[512]{0:T(512)S(1)} %add_reduce_fusion), kind=kOutput, calls=%fused_computation.3 | convolution fusion | flops 2149580800 | bytes 8394752 | tf_op jit(solution)/shard_map/dot_general | solution.py:14
  148.3 43.6 %all-to-all-done.3 = bf16[32,16,2048]{2,1,0:T(8,128)(2,1)S(1)} async-done(((bf16[32,16,2048]{2,1,0:T(8,128)(2,1)}), bf16[32,16,2048]{2,1,0:T(8,128)(2,1)S(1)}, u32[]{:S(2)}, u32[]{:S(2)}) %all-to-all-start.3) | async-done | bytes 2097184 | tf_op jit(solution)/shard_map/all_to_all | solution.py:21
  191.8 1.3 copy-done.2
  193.2 2.9 %all-to-all-start.1 = ((bf16[32,16,2048]{2,1,0:T(8,128)(2,1)}), bf16[32,16,2048]{2,1,0:T(8,128)(2,1)S(1)}, u32[]{:S(2)}, u32[]{:S(2)}) async-start(bf16[32,16,2048]{2,1,0:T(8,128)(2,1)} %bitcast.35), calls=%async_computation.1 | async-start | bytes 4194304 | tf_op jit(solution)/shard_map/all_to_all | solution.py:21
  196.1 0.0 copy-start.12
  196.1 0.0 copy-start.14
  196.1 4.9 %fusion.44 = f32[1024,2048]{1,0:T(8,128)S(1)} fusion(bf16[512,2048]{1,0:T(8,128)(2,1)} %bitcast.31, f32[512,1024]{1,0:T(8,128)} %add_divide_fusion, s32[1024]{0:T(1024)S(1)} %add_select_fusion.2, s32[512]{0:T(512)S(1)} %add_reduce_fusion), kind=kOutput, calls=%fused_computation.87 | convolution fusion | flops 2148532224 | bytes 12589056 | tf_op jit(solution)/shard_map/dot_general | solution.py:14
  201.0 0.0 copy-done.12
  201.0 0.0 copy-done.14
  201.0 4.7 %add_convert_fusion = bf16[1024,2048]{1,0:T(8,128)(2,1)} fusion(f32[1024,2048]{1,0:T(8,128)S(1)} %fusion.44, bf16[512,1024]{1,0:T(8,128)(2,1)S(1)} %copy-done.14, bf16[512,2048]{1,0:T(8,128)(2,1)S(1)} %copy-done.12), kind=kOutput, calls=%fused_computation | convolution fusion | flops 2151677952 | bytes 15728640 | tf_op jit(solution)/shard_map/dot_general | solution.py:14
  205.7 8.3 %fusion.10 = (f32[128]{0:T(128)S(1)}, f32[128,2048]{1,0:T(8,128)}) fusion(bf16[128,2048]{1,0:T(8,128)(2,1)S(1)} %copy-done, f32[128]{0:T(128)S(1)} %add_rsqrt_fusion, f32[2048]{0:T(1024)S(1)} %copy-done.6, bf16[2048,2048]{1,0:T(8,128)(2,1)} %all-gather.2.cloned.1.call-done, bf16[512,2048]{1,0:T(8,128)(2,1)} %bitcast.32, s32[128]{0:T(128)S(1)} %get-tuple-element.9, ...), kind=kOutput, calls=%fused_computation.27 | convolution fusion | flops 1344274304 | bytes 12068864 | tf_op jit(solution)/shard_map/dot_general | solution.py:14
  214.0 32.0 %all-to-all-done.1 = bf16[32,16,2048]{2,1,0:T(8,128)(2,1)S(1)} async-done(((bf16[32,16,2048]{2,1,0:T(8,128)(2,1)}), bf16[32,16,2048]{2,1,0:T(8,128)(2,1)S(1)}, u32[]{:S(2)}, u32[]{:S(2)}) %all-to-all-start.1) | async-done | bytes 2097184 | tf_op jit(solution)/shard_map/all_to_all | solution.py:21
  246.0 0.5 convolution_multiply_fusion.2
  246.5 0.0 copy-start.3
  246.5 1.5 fusion.1
  248.0 0.0 copy-done.3
  248.0 1.3 fusion.13
  (13 shorter events, 0.1 us)
Async XLA Ops:
  7.2 0.8 copy-start.7
  7.2 2.2 copy-start
  7.2 2.4 copy-start.6
  7.2 103.8 %all-gather.2.cloned.1.call-start = ((), (), s32[]{:S(2)}) async-start(), calls=%async_computation.4 | async-start | bytes 10485760 | tf_op jit(solution)/shard_map/all_gather | solution.py:41
  12.1 7.3 %copy-start.8 = (f32[128,2]{0,1:T(2,128)S(1)}, f32[128,2]{0,1:T(2,128)}, u32[]{:S(2)}) copy-start(f32[128,2]{0,1:T(2,128)} %param.12) | copy-start | bytes 3076
  12.1 7.6 %copy-start.5 = (bf16[128,2048]{1,0:T(8,128)(2,1)S(1)}, bf16[128,2048]{1,0:T(8,128)(2,1)}, u32[]{:S(2)}) copy-start(bf16[128,2048]{1,0:T(8,128)(2,1)} %param.13) | copy-start | bytes 1572868
  12.1 60.3 %all-to-all-start = ((bf16[32,16,2176]{2,1,0:T(8,128)(2,1)}), bf16[32,16,2176]{2,1,0:T(8,128)(2,1)S(1)}, u32[]{:S(2)}, u32[]{:S(2)}) async-start(bf16[32,16,2176]{2,1,0:T(8,128)(2,1)} %bitcast.2), calls=%async_computation | async-start | bytes 4456448 | tf_op jit(solution)/shard_map/all_to_all | solution.py:21
  72.4 1.4 copy-start.4
  73.8 52.8 %all-to-all-start.2 = ((bf16[32,16,2048]{2,1,0:T(8,128)(2,1)}), bf16[32,16,2048]{2,1,0:T(8,128)(2,1)S(1)}, u32[]{:S(2)}, u32[]{:S(2)}) async-start(bf16[32,16,2048]{2,1,0:T(8,128)(2,1)} %bitcast.6), calls=%async_computation.2 | async-start | bytes 4194304 | tf_op jit(solution)/shard_map/all_to_all | solution.py:21
  111.0 10.1 %copy-start.9 = (bf16[1024,2048]{1,0:T(8,128)(2,1)S(1)}, bf16[1024,2048]{1,0:T(8,128)(2,1)}, u32[]{:S(2)}) copy-start(bf16[1024,2048]{1,0:T(8,128)(2,1)} %param.10) | copy-start | bytes 12582916
  119.7 1.4 copy-start.11
  126.6 6.2 %copy-start.1 = (bf16[32,16,2048]{2,1,0:T(8,128)(2,1)}, bf16[32,16,2048]{2,1,0:T(8,128)(2,1)S(1)}, u32[]{:S(2)}) copy-start(bf16[32,16,2048]{2,1,0:T(8,128)(2,1)S(1)} %all-to-all-done.2) | copy-start | bytes 6291460
  126.6 6.2 %copy-start.10 = (bf16[1024,2048]{1,0:T(8,128)(2,1)S(1)}, bf16[1024,2048]{1,0:T(8,128)(2,1)}, u32[]{:S(2)}) copy-start(bf16[1024,2048]{1,0:T(8,128)(2,1)} %param.10) | copy-start | bytes 12582916
  132.9 3.7 %copy-start.13 = (bf16[512,1024]{1,0:T(8,128)(2,1)}, bf16[512,1024]{1,0:T(8,128)(2,1)S(1)}, u32[]{:S(2)}) copy-start(bf16[512,1024]{1,0:T(8,128)(2,1)S(1)} %fusion.3) | copy-start | bytes 3145732
  136.6 55.3 %all-to-all-start.3 = ((bf16[32,16,2048]{2,1,0:T(8,128)(2,1)}), bf16[32,16,2048]{2,1,0:T(8,128)(2,1)S(1)}, u32[]{:S(2)}, u32[]{:S(2)}) async-start(bf16[32,16,2048]{2,1,0:T(8,128)(2,1)} %bitcast.36), calls=%async_computation.3 | async-start | bytes 4194304 | tf_op jit(solution)/shard_map/all_to_all | solution.py:21
  191.8 1.3 copy-start.2
  193.2 52.8 %all-to-all-start.1 = ((bf16[32,16,2048]{2,1,0:T(8,128)(2,1)}), bf16[32,16,2048]{2,1,0:T(8,128)(2,1)S(1)}, u32[]{:S(2)}, u32[]{:S(2)}) async-start(bf16[32,16,2048]{2,1,0:T(8,128)(2,1)} %bitcast.35), calls=%async_computation.1 | async-start | bytes 4194304 | tf_op jit(solution)/shard_map/all_to_all | solution.py:21
  196.1 4.9 %copy-start.12 = (bf16[512,2048]{1,0:T(8,128)(2,1)S(1)}, bf16[512,2048]{1,0:T(8,128)(2,1)}, u32[]{:S(2)}) copy-start(bf16[512,2048]{1,0:T(8,128)(2,1)} %copy-done.11) | copy-start | bytes 6291460
  196.1 4.9 %copy-start.14 = (bf16[512,1024]{1,0:T(8,128)(2,1)S(1)}, bf16[512,1024]{1,0:T(8,128)(2,1)}, u32[]{:S(2)}) copy-start(bf16[512,1024]{1,0:T(8,128)(2,1)} %copy-done.13) | copy-start | bytes 3145732
  246.5 1.5 copy-start.3
Sparse Core Ops, SparseCore 0:
  9.6 101.3 all-gather.1

commit v3 on v1

v3 whole, which is shorter than its diff:
```python
import jax
import jax.numpy as jnp
from jax import lax
from jax.sharding import Mesh, PartitionSpec as P

BLOCK = 64
LANES = 128
AXES = ("dp", "half", "near")
NEAR = ("dp", "near")
BF = jnp.bfloat16
F32 = jnp.float32


def dot(left, right, left_dim=1, right_dim=0):
    return lax.dot_general(
        left, right, (((left_dim,), (right_dim,)), ((), ())), preferred_element_type=F32
    )


def exchange(rows, owner_count):
    slots, features = rows.shape
    out = lax.all_to_all(
        rows.reshape(owner_count, slots // owner_count, features),
        NEAR,
        split_axis=0,
        concat_axis=0,
        tiled=True,
    )
    return out.reshape(slots, features)


def across(rows):
    return lax.ppermute(rows, "half", [(0, 1), (1, 0)])


def slots_of(block_ids, lookup_weights, near_count, capacity, span_blocks):
    token_count, top_count = block_ids.shape
    pair_count = token_count * top_count
    owner_of = block_ids // span_blocks
    half_of = owner_of // lax.axis_size("near") % 2
    here = half_of == lax.axis_index("half")
    near_of = owner_of // (2 * lax.axis_size("near")) * lax.axis_size("near")
    near_of = near_of + owner_of % lax.axis_size("near")
    near_of = jnp.where(here, near_of, near_count).reshape(pair_count)
    earlier = (
        jnp.arange(pair_count)[:, None] > jnp.arange(pair_count)[None, :]
    ).astype(BF)
    hits = near_of[:, None] == jnp.arange(near_count, dtype=jnp.int32)[None, :]
    ranks = dot(earlier, hits.astype(BF))
    slot_of = jnp.sum(jnp.where(hits, ranks, 0.0), axis=1).astype(jnp.int32)
    target = (near_of * capacity + slot_of).reshape(token_count, top_count)
    slot_ids = jnp.arange(near_count * capacity, dtype=jnp.int32)
    picks = [(target[:, k][None, :] == slot_ids[:, None]) for k in range(top_count)]
    pick_rows = sum(p.astype(BF) for p in picks)
    slot_weight = sum(
        jnp.sum(jnp.where(p, lookup_weights[:, k][None, :], 0.0), axis=1, keepdims=True)
        for k, p in enumerate(picks)
    )
    local_next = block_ids % span_blocks + 1
    slot_block = sum(
        jnp.sum(jnp.where(p, local_next[:, k][None, :], 0), axis=1, keepdims=True)
        for k, p in enumerate(picks)
    )
    return picks, pick_rows, slot_weight, slot_block


def body(tokens, norm_gain, query_weight, values, blocks, weights, out_cotangent):
    token_count, features = tokens.shape
    top_count = blocks.shape[1]
    value_rows = values.shape[0]
    span_blocks = value_rows // BLOCK
    near_count = lax.axis_size("dp") * lax.axis_size("near")
    capacity = token_count * top_count // near_count
    score_scale = float(features) ** (-0.5)
    weight_full = lax.all_gather(query_weight, "dp", axis=1, tiled=True)

    exact_tokens = tokens.astype(F32)
    rms_rows = lax.rsqrt(jnp.mean(exact_tokens * exact_tokens, axis=1, keepdims=True) + 1e-06)
    unit_rows = exact_tokens * rms_rows
    normed = (unit_rows * norm_gain).astype(BF)

    facts = across(jnp.concatenate([blocks.astype(F32), weights], axis=1))
    far_blocks = facts[:, :top_count].astype(jnp.int32)
    far_weights = facts[:, top_count:]
    far_normed = across(normed)
    far_cot = across(out_cotangent)

    row_block = jnp.arange(value_rows, dtype=jnp.int32) // BLOCK

    def send(block_ids, lookup_weights, normed_part, cot_part):
        picks, pick_rows, slot_weight, slot_block = slots_of(
            block_ids, lookup_weights, near_count, capacity, span_blocks
        )
        load = jnp.concatenate(
            [
                dot(pick_rows, normed_part).astype(BF),
                (slot_weight * dot(pick_rows, cot_part)).astype(BF),
                jnp.broadcast_to(slot_block.astype(BF), (slot_block.shape[0], LANES)),
            ],
            axis=1,
        )
        return picks, pick_rows, exchange(load, near_count)

    def look_up(arrived):
        normed_rows = arrived[:, :features]
        cot_rows = arrived[:, features : 2 * features]
        block_here = arrived[:, 2 * features : 2 * features + 1].astype(jnp.int32) - 1
        in_block = block_here == row_block[None, :]
        query_rows = dot(normed_rows, weight_full).astype(BF)
        sigmoid_of = jax.nn.sigmoid(dot(query_rows, values, 1, 1) * score_scale)
        gate_values = jnp.where(in_block, sigmoid_of, 0.0).astype(BF)
        cot_scores = dot(cot_rows, values, 1, 1)
        score_grads = jnp.where(
            in_block, cot_scores * sigmoid_of * (1.0 - sigmoid_of) * score_scale, 0.0
        ).astype(BF)
        back = jnp.concatenate(
            [dot(gate_values, values).astype(BF), dot(score_grads, values).astype(BF)], axis=1
        )
        grads = dot(gate_values, cot_rows, 0, 0) + dot(score_grads, query_rows, 0, 0)
        return back, grads

    def take(returned, lookup_weights, picks, pick_rows):
        mixed = sum(
            lookup_weights[:, k][:, None] * dot(p.astype(BF), returned[:, :features], 0, 0)
            for k, p in enumerate(picks)
        )
        return mixed, dot(pick_rows, returned[:, features:], 0, 0)

    picks, pick_rows, arrived = send(blocks, weights, normed, out_cotangent)
    far_picks, far_pick_rows, far_arrived = send(far_blocks, far_weights, far_normed, far_cot)
    back, grads = look_up(arrived)
    far_back, far_grads = look_up(far_arrived)
    far_mixed, far_query = take(
        exchange(far_back, near_count), far_weights, far_picks, far_pick_rows
    )
    mixed, query_sum = take(exchange(back, near_count), weights, picks, pick_rows)
    other_query = across(far_query.astype(BF))
    other_mixed = across(far_mixed.astype(BF))
    grad_values = (grads + far_grads).astype(BF)

    layer_out = exact_tokens + (mixed + other_mixed.astype(F32))
    query_grad = (query_sum + other_query.astype(F32)).astype(BF)
    unit_grad = dot(query_grad, weight_full, 1, 1) * norm_gain
    grad_tokens = out_cotangent.astype(F32) + rms_rows * (
        unit_grad - unit_rows * jnp.mean(unit_grad * unit_rows, axis=1, keepdims=True)
    )
    return (layer_out, grad_tokens, grad_values)


def solution(mesh):
    rows = P(AXES, None)
    dp_size, mem_size = mesh.devices.shape
    halves = Mesh(mesh.devices.reshape(dp_size, 2, mem_size // 2), AXES)
    return jax.shard_map(
        body,
        mesh=halves,
        in_specs=(rows, P(), P(None, "dp"), rows, rows, rows, rows),
        out_specs=(rows, rows, rows),
        check_vma=False,
    )
```

time: 320 us -> 254 us (0.79)
  blocking collectives: 104 us -> 0 us
  matrix products: 52 us -> 64.9 us
  other arithmetic: 2.51 us -> 15.1 us
  starting transfers between devices: 16.5 us -> 27.4 us
    all_gather x1 -> x0, blocking collectives: 104 us -> none  [body(): all_blocks = lax.all_gather(blocks, AXES, axis=0, tiled=True)]
    ppermute x0 -> x5, waiting for transfers between devices: none -> 77.2 us  [across(): return lax.ppermute(rows, 'half', [(0, 1), (1, 0)])]
    all_to_all x4, waiting for transfers between devices: 123 us -> 49 us  [exchange(): lax.all_to_all(rows.reshape(owner_count, slots // owner_count, features),...]
    dot_general x14 -> x26, matrix products: 52 us -> 64.9 us  [dot(): lax.dot_general(left, right, (((left_dim,), (right_dim,)), ((), ())), pre...]
    ppermute x0 -> x5, starting transfers between devices: none -> 10 us  [across(): return lax.ppermute(rows, 'half', [(0, 1), (1, 0)])]
    concatenate x0 -> x5, other arithmetic: none -> 6.81 us  [the longest x2 3.08 us: send(): jnp.concatenate([dot(pick_rows, normed_part).astype(BF), (slot_weight * d...]
  transfers between devices with their start and end apart: 5 -> 10, of which waited for: 3 -> 7; matrix products, arithmetic and copies ran while one was open for 14% -> 31% of each run, Pallas kernels for 0% -> 0%
where the time goes in v3:
time: 254 us; the launch traced here: 253 us
  waiting for transfers between devices  127 us (50%)
  matrix products  64.9 us (26%)
  starting transfers between devices  27.4 us (11%)
  other arithmetic  15.1 us (6%)
  between operations  14.6 us (6%)
  local copies, waits for them, and re-layouts  4.13 us (2%)
    ppermute x5, waiting for transfers between devices, across(): return lax.ppermute(rows, 'half', [(0, 1), (1, 0)])  77.2 us
    dot_general x26, matrix products, dot(): lax.dot_general(left, right, (((left_dim,), (right_dim,)), ((), ())), pre...  64.9 us
    all_to_all x4, waiting for transfers between devices, exchange(): lax.all_to_all(rows.reshape(owner_count, slots // owner_count, features),...  49 us
    all_to_all x4, starting transfers between devices, exchange(): lax.all_to_all(rows.reshape(owner_count, slots // owner_count, features),...  17.4 us
    ppermute x5, starting transfers between devices, across(): return lax.ppermute(rows, 'half', [(0, 1), (1, 0)])  10 us
  transfers between devices with their start and end apart: 10, of which 7 were waited for; matrix products, arithmetic and copies ran while one was open for 31% of the time, Pallas kernels for 0%

profile of v3, /device:TPU:0, one launch (start us, length us, event | category | flops | bytes accessed | tf_op | source)
XLA Modules:
  0.0 252.9 jit_solution(10735307929829410145)
XLA Ops:
  7.2 0.7 all-gather.2.cloned.1.call-update
  7.9 0.7 convert_element_type.146
  8.6 0.7 pad_maximum_fusion.4
  9.4 4.1 %collective-permute-start = (f32[128,4]{1,0:T(8,128)S(1)}, f32[128,4]{1,0:T(8,128)S(1)}, u32[]{:S(2)}, u32[]{:S(2)}) collective-permute-start(f32[128,4]{1,0:T(8,128)S(1)} %copy.45), channel_id=1, source_target_pairs={{0,4},{4,0},{1,5},{5,1},{2,6},{6,2},{3,7},{7,3},{8,12},{12,8},{9,1... | collective-permute-start | bytes 6152 | tf_op jit(solution)/shard_map/ppermute | solution.py:33
  13.5 1.2 fusion.29
  14.7 1.2 fusion.24
  16.1 2.9 %collective-permute-start.2 = (bf16[128,2048]{1,0:T(8,128)(2,1)}, bf16[128,2048]{1,0:T(8,128)(2,1)S(1)}, u32[]{:S(2)}, u32[]{:S(2)}) collective-permute-start(bf16[128,2048]{1,0:T(8,128)(2,1)} %param.13), channel_id=1, source_target_pairs={{0,4},{4,0},{1,5},{5,1},{2,6},{6,2},{3,7},{7,3},{8,12},{12,8},{9,1... | collective-permute-start | bytes 1572872 | tf_op jit(solution)/shard_map/ppermute | solution.py:33
  19.0 0.2 fusion.69
  19.3 0.2 fusion.21
  19.7 0.2 slice_reduce_fusion
  19.9 0.2 slice_reduce_fusion.3
  20.2 0.2 slice_reduce_fusion.2
  20.7 33.2 %collective-permute-done.1 = bf16[128,2048]{1,0:T(8,128)(2,1)S(1)} collective-permute-done((bf16[128,2048]{1,0:T(8,128)(2,1)S(1)}, bf16[128,2048]{1,0:T(8,128)(2,1)S(1)}, u32[]{:S(2)}, u32[]{:S(2)}) %collective-permute-start.1) | collective-permute-done | bytes 524320 | tf_op jit(solution)/shard_map/ppermute | solution.py:33
  54.0 0.4 convolution_convert_fusion
  54.4 9.6 %collective-permute-done.2 = bf16[128,2048]{1,0:T(8,128)(2,1)S(1)} collective-permute-done((bf16[128,2048]{1,0:T(8,128)(2,1)}, bf16[128,2048]{1,0:T(8,128)(2,1)S(1)}, u32[]{:S(2)}, u32[]{:S(2)}) %collective-permute-start.2) | collective-permute-done | bytes 524320 | tf_op jit(solution)/shard_map/ppermute | solution.py:33
  64.0 0.4 fusion.1
  64.6 1.5 pad_maximum_fusion.1
  66.1 4.0 %all-to-all-start.2 = ((bf16[16,16,4224]{2,1,0:T(8,128)(2,1)}), bf16[16,16,4224]{2,1,0:T(8,128)(2,1)S(1)}, u32[]{:S(2)}, u32[]{:S(2)}) async-start(bf16[16,16,4224]{2,1,0:T(8,128)(2,1)} %bitcast.6), calls=%async_computation.2 | async-start | bytes 4325376 | tf_op jit(solution)/shard_map/all_to_all | solution.py:22
  70.2 0.1 copy.43
  70.3 0.2 fusion.62
  70.7 0.2 fusion.20
  71.0 0.2 slice_reduce_fusion.8
  71.2 0.2 select_reduce_fusion.6
  71.4 0.2 slice_reduce_fusion.6
  71.6 0.2 select_reduce_fusion.4
  71.8 1.5 convolution_convert_fusion.1
  73.2 0.4 fusion
  73.8 1.6 pad_maximum_fusion
  75.3 23.5 %all-to-all-done.2 = bf16[16,16,4224]{2,1,0:T(8,128)(2,1)S(1)} async-done(((bf16[16,16,4224]{2,1,0:T(8,128)(2,1)}), bf16[16,16,4224]{2,1,0:T(8,128)(2,1)S(1)}, u32[]{:S(2)}, u32[]{:S(2)}) %all-to-all-start.2) | async-done | bytes 2162720 | tf_op jit(solution)/shard_map/all_to_all | solution.py:22
  98.8 4.4 %all-to-all-start = ((bf16[16,16,4224]{2,1,0:T(8,128)(2,1)}), bf16[16,16,4224]{2,1,0:T(8,128)(2,1)}, u32[]{:S(2)}, u32[]{:S(2)}) async-start(bf16[16,16,4224]{2,1,0:T(8,128)(2,1)} %bitcast.2), calls=%async_computation | async-start | bytes 4325376 | tf_op jit(solution)/shard_map/all_to_all | solution.py:22
  103.4 5.9 %convolution_convert_fusion.6 = bf16[256,2048]{1,0:T(8,128)(2,1)S(1)} fusion(bf16[2048,2048]{1,0:T(8,128)(2,1)} %all-gather.2.cloned.1.call-done, bf16[256,4224]{1,0:T(8,128)(2,1)S(1)} %bitcast.41), kind=kOutput, calls=%fused_computation.11 | convolution fusion | flops 2148007936 | bytes 10485760 | tf_op jit(solution)/shard_map/dot_general | solution.py:15
  109.3 1.0 copy-done.9
  110.3 1.5 fusion.17
  111.9 1.4 fusion.19
  113.3 1.3 convolution_convert_fusion.2
  114.6 1.3 convolution_convert_fusion.3
  115.9 1.5 pad_maximum_fusion.3
  117.4 14.4 %all-to-all-done = bf16[16,16,4224]{2,1,0:T(8,128)(2,1)} async-done(((bf16[16,16,4224]{2,1,0:T(8,128)(2,1)}), bf16[16,16,4224]{2,1,0:T(8,128)(2,1)}, u32[]{:S(2)}, u32[]{:S(2)}) %all-to-all-start) | async-done | bytes 2162720 | tf_op jit(solution)/shard_map/all_to_all | solution.py:22
  131.9 4.3 %all-to-all-start.3 = ((bf16[16,16,4096]{2,1,0:T(8,128)(2,1)}), bf16[16,16,4096]{2,1,0:T(8,128)(2,1)S(1)}, u32[]{:S(2)}, u32[]{:S(2)}) async-start(bf16[16,16,4096]{2,1,0:T(8,128)(2,1)} %bitcast.39), calls=%async_computation.3 | async-start | bytes 4194304 | tf_op jit(solution)/shard_map/all_to_all | solution.py:22
  136.2 1.0 add_reduce_fusion.1
  137.2 6.2 %convolution_convert_fusion.7 = bf16[256,2048]{1,0:T(8,128)(2,1)S(1)} fusion(bf16[2048,2048]{1,0:T(8,128)(2,1)} %all-gather.2.cloned.1.call-done, bf16[256,4224]{1,0:T(8,128)(2,1)} %bitcast.3), kind=kOutput, calls=%fused_computation.12 | convolution fusion | flops 2148007936 | bytes 10485760 | tf_op jit(solution)/shard_map/dot_general | solution.py:15
  143.4 1.0 copy-done.8
  144.4 1.5 fusion.15
  145.9 3.0 %fusion.18 = bf16[256,1024]{1,0:T(8,128)(2,1)S(1)} fusion(f32[256,1024]{1,0:T(8,128)S(1)} %fusion.15, bf16[1024,2048]{1,0:T(8,128)(2,1)S(1)} %copy-done.17, bf16[256,4224]{1,0:T(8,128)(2,1)} %bitcast.3, s32[1024]{0:T(1024)S(1)} %add_select_fusion.12, s32[256]{0:T(256)S(1)} %add_reduce_fusion.1), kind=kOutput, calls=%fused_computation.48 | convolution fusion | flops 1075576832 | bytes 6820864 | tf_op jit(solution)/shard_map/dot_general | solution.py:15
  148.9 1.3 convolution_convert_fusion.4
  150.2 1.3 convolution_convert_fusion.5
  151.5 1.5 pad_maximum_fusion.2
  153.0 11.1 %all-to-all-done.3 = bf16[16,16,4096]{2,1,0:T(8,128)(2,1)S(1)} async-done(((bf16[16,16,4096]{2,1,0:T(8,128)(2,1)}), bf16[16,16,4096]{2,1,0:T(8,128)(2,1)S(1)}, u32[]{:S(2)}, u32[]{:S(2)}) %all-to-all-start.3) | async-done | bytes 2097184 | tf_op jit(solution)/shard_map/all_to_all | solution.py:22
  164.1 4.7 %all-to-all-start.1 = ((bf16[16,16,4096]{2,1,0:T(8,128)(2,1)}), bf16[16,16,4096]{2,1,0:T(8,128)(2,1)}, u32[]{:S(2)}, u32[]{:S(2)}) async-start(bf16[16,16,4096]{2,1,0:T(8,128)(2,1)} %bitcast.38), calls=%async_computation.1 | async-start | bytes 4194304 | tf_op jit(solution)/shard_map/all_to_all | solution.py:22
  168.8 5.8 %fusion.125 = f32[1024,2048]{1,0:T(8,128)} fusion(bf16[256,1024]{1,0:T(8,128)(2,1)S(1)} %fusion.18, bf16[256,2048]{1,0:T(8,128)(2,1)} %copy-done.8), kind=kOutput, calls=%fused_computation.213 | convolution fusion | flops 1073741824 | bytes 9961472 | tf_op jit(solution)/shard_map/dot_general | solution.py:15
  174.6 2.7 %fusion.44 = f32[1024,2048]{1,0:T(8,128)S(1)} fusion(bf16[256,4224]{1,0:T(8,128)(2,1)} %bitcast.3, f32[256,1024]{1,0:T(8,128)S(1)} %copy-done.7, s32[1024]{0:T(1024)S(1)} %add_select_fusion.12, s32[256]{0:T(256)S(1)} %add_reduce_fusion.1), kind=kOutput, calls=%fused_computation.78 | convolution fusion | flops 1074266112 | bytes 10490880 | tf_op jit(solution)/shard_map/dot_general | solution.py:15
  177.3 5.9 %fusion.39 = f32[1024,2048]{1,0:T(8,128)} fusion(bf16[256,4224]{1,0:T(8,128)(2,1)} %bitcast.43, f32[256,1024]{1,0:T(8,128)S(1)} %copy-done.5, s32[1024]{0:T(1024)S(1)} %add_select_fusion.12, s32[256]{0:T(256)S(1)} %add_reduce_fusion), kind=kOutput, calls=%fused_computation.73 | convolution fusion | flops 1074266112 | bytes 10490880 | tf_op jit(solution)/shard_map/dot_general | solution.py:15
  183.3 9.8 %add_convert_fusion = bf16[1024,2048]{1,0:T(8,128)(2,1)} fusion(f32[1024,2048]{1,0:T(8,128)} %fusion.39, f32[1024,2048]{1,0:T(8,128)S(1)} %fusion.44, f32[1024,2048]{1,0:T(8,128)} %fusion.125, bf16[256,1024]{1,0:T(8,128)(2,1)S(1)} %copy-done.12, bf16[256,2048]{1,0:T(8,128)(2,1)S(1)} %copy-done.10), kind=kOutput, calls=%fused_computation | convolution fusion | flops 1082130432 | bytes 30932992 | tf_op jit(solution)/shard_map/dot_general | solution.py:15
  193.0 1.1 convolution_convert_fusion.8
  194.2 1.4 collective-permute-start.4
  195.6 0.3 fusion.37
  196.0 1.2 add_convert_fusion.2
  197.2 1.5 collective-permute-start.3
  198.6 1.6 convolution_multiply_fusion.4
  200.2 1.6 fusion.2
  201.8 30.2 %collective-permute-done.4 = bf16[128,2048]{1,0:T(8,128)(2,1)} collective-permute-done((bf16[128,2048]{1,0:T(8,128)(2,1)}, bf16[128,2048]{1,0:T(8,128)(2,1)}, u32[]{:S(2)}, u32[]{:S(2)}) %collective-permute-start.4) | collective-permute-done | bytes 524320 | tf_op jit(solution)/shard_map/ppermute | solution.py:33
  232.0 7.1 %fusion.25 = (f32[128]{0:T(128)S(1)}, f32[128,2048]{1,0:T(8,128)S(1)}) fusion(bf16[128,2048]{1,0:T(8,128)(2,1)S(1)} %copy-done, f32[128]{0:T(128)S(1)} %add_rsqrt_fusion, f32[2048]{0:T(1024)S(1)} %copy-done.13, bf16[2048,2048]{1,0:T(8,128)(2,1)} %all-gather.2.cloned.1.call-done, bf16[128,2048]{1,0:T(8,128)(2,1)} %collective-permute-done.4, ...), kind=kOutput, calls=%fused_computation.57 | convolution fusion | flops 1210318720 | bytes 11544576 | tf_op jit(solution)/shard_map/dot_general | solution.py:15
  239.1 4.1 %collective-permute-done.3 = bf16[128,2048]{1,0:T(8,128)(2,1)} collective-permute-done((bf16[128,2048]{1,0:T(8,128)(2,1)}, bf16[128,2048]{1,0:T(8,128)(2,1)}, u32[]{:S(2)}, u32[]{:S(2)}) %collective-permute-start.3) | collective-permute-done | bytes 524320 | tf_op jit(solution)/shard_map/ppermute | solution.py:33
  243.2 2.8 %fusion.28 = (f32[128,2048]{1,0:T(8,128)}, f32[128,2048]{1,0:T(8,128)}) fusion(f32[128,2048]{1,0:T(8,128)S(1)} %get-tuple-element.22, bf16[128,2048]{1,0:T(8,128)(2,1)S(1)} %copy-done, bf16[128,2048]{1,0:T(8,128)(2,1)S(1)} %copy-done.2, f32[128]{0:T(128)S(1)} %broadcast_multiply_fusion, f32[128]{0:T(128)S(1)} %add_rsqrt_fusion, f32[128,2048]{1,0:T(8,128)S(1)} %fusion.2, ...), kind=kLoop, calls=%fused_computation.60 | loop fusion | flops 2621440 | bytes 5768192 | tf_op jit(solution)/shard_map/add | solution.py:144
  (65 shorter events, 1.9 us)
Async XLA Ops:
  7.2 96.2 %all-gather.2.cloned.1.call-start = ((), (), s32[]{:S(2)}) async-start(), calls=%async_computation.4 | async-start | bytes 10485760 | tf_op jit(solution)/shard_map/all_gather | solution.py:75
  9.4 9.6 %collective-permute-start = (f32[128,4]{1,0:T(8,128)S(1)}, f32[128,4]{1,0:T(8,128)S(1)}, u32[]{:S(2)}, u32[]{:S(2)}) collective-permute-start(f32[128,4]{1,0:T(8,128)S(1)} %copy.45), channel_id=1, source_target_pairs={{0,4},{4,0},{1,5},{5,1},{2,6},{6,2},{3,7},{7,3},{8,12},{12,8},{9,1... | collective-permute-start | bytes 6152 | tf_op jit(solution)/shard_map/ppermute | solution.py:33
  16.0 50.1 %copy-start.3 = (bf16[128,2048]{1,0:T(8,128)(2,1)}, bf16[128,2048]{1,0:T(8,128)(2,1)S(1)}, u32[]{:S(2)}) copy-start(bf16[128,2048]{1,0:T(8,128)(2,1)S(1)} %fusion.24) | copy-start | bytes 1572868
  16.0 38.0 %collective-permute-start.1 = (bf16[128,2048]{1,0:T(8,128)(2,1)S(1)}, bf16[128,2048]{1,0:T(8,128)(2,1)S(1)}, u32[]{:S(2)}, u32[]{:S(2)}) collective-permute-start(bf16[128,2048]{1,0:T(8,128)(2,1)S(1)} %fusion.24), channel_id=1, source_target_pairs={{0,4},{4,0},{1,5},{5,1},{2,6},{6,2},{3,7},{7,3},{8,12},{12,8},{9,1... | collective-permute-start | bytes 1572872 | tf_op jit(solution)/shard_map/ppermute | solution.py:33
  16.1 48.0 %collective-permute-start.2 = (bf16[128,2048]{1,0:T(8,128)(2,1)}, bf16[128,2048]{1,0:T(8,128)(2,1)S(1)}, u32[]{:S(2)}, u32[]{:S(2)}) collective-permute-start(bf16[128,2048]{1,0:T(8,128)(2,1)} %param.13), channel_id=1, source_target_pairs={{0,4},{4,0},{1,5},{5,1},{2,6},{6,2},{3,7},{7,3},{8,12},{12,8},{9,1... | collective-permute-start | bytes 1572872 | tf_op jit(solution)/shard_map/ppermute | solution.py:33
  64.6 5.5 %copy-start.14 = (s32[128,2]{0,1:T(2,128)S(1)}, s32[128,2]{0,1:T(2,128)}, u32[]{:S(2)}) copy-start(s32[128,2]{0,1:T(2,128)} %param.11) | copy-start | bytes 3076
  64.6 6.7 %copy-start.15 = (f32[128,2]{0,1:T(2,128)S(1)}, f32[128,2]{0,1:T(2,128)}, u32[]{:S(2)}) copy-start(f32[128,2]{0,1:T(2,128)} %param.12) | copy-start | bytes 3076
  66.1 7.1 %copy-start.2 = (bf16[128,2048]{1,0:T(8,128)(2,1)S(1)}, bf16[128,2048]{1,0:T(8,128)(2,1)}, u32[]{:S(2)}) copy-start(bf16[128,2048]{1,0:T(8,128)(2,1)} %param.13) | copy-start | bytes 1572868
  66.1 32.7 %all-to-all-start.2 = ((bf16[16,16,4224]{2,1,0:T(8,128)(2,1)}), bf16[16,16,4224]{2,1,0:T(8,128)(2,1)S(1)}, u32[]{:S(2)}, u32[]{:S(2)}) async-start(bf16[16,16,4224]{2,1,0:T(8,128)(2,1)} %bitcast.6), calls=%async_computation.2 | async-start | bytes 4325376 | tf_op jit(solution)/shard_map/all_to_all | solution.py:22
  98.8 13.0 %copy-start.1 = (bf16[16,16,4224]{2,1,0:T(8,128)(2,1)}, bf16[16,16,4224]{2,1,0:T(8,128)(2,1)S(1)}, u32[]{:S(2)}) copy-start(bf16[16,16,4224]{2,1,0:T(8,128)(2,1)S(1)} %all-to-all-done.2) | copy-start | bytes 6488068
  98.8 33.1 %all-to-all-start = ((bf16[16,16,4224]{2,1,0:T(8,128)(2,1)}), bf16[16,16,4224]{2,1,0:T(8,128)(2,1)}, u32[]{:S(2)}, u32[]{:S(2)}) async-start(bf16[16,16,4224]{2,1,0:T(8,128)(2,1)} %bitcast.2), calls=%async_computation | async-start | bytes 4325376 | tf_op jit(solution)/shard_map/all_to_all | solution.py:22
  103.4 6.9 %copy-start.16 = (bf16[1024,2048]{1,0:T(8,128)(2,1)S(1)}, bf16[1024,2048]{1,0:T(8,128)(2,1)}, u32[]{:S(2)}) copy-start(bf16[1024,2048]{1,0:T(8,128)(2,1)} %param.10) | copy-start | bytes 12582916
  109.3 1.0 copy-start.9
  111.9 2.7 %copy-start.4 = (f32[256,1024]{1,0:T(8,128)}, f32[256,1024]{1,0:T(8,128)S(1)}, u32[]{:S(2)}) copy-start(f32[256,1024]{1,0:T(8,128)S(1)} %fusion.17) | copy-start | bytes 3145732
  113.3 2.6 %copy-start.11 = (bf16[256,1024]{1,0:T(8,128)(2,1)}, bf16[256,1024]{1,0:T(8,128)(2,1)S(1)}, u32[]{:S(2)}) copy-start(bf16[256,1024]{1,0:T(8,128)(2,1)S(1)} %fusion.19) | copy-start | bytes 1572868
  131.9 32.2 %all-to-all-start.3 = ((bf16[16,16,4096]{2,1,0:T(8,128)(2,1)}), bf16[16,16,4096]{2,1,0:T(8,128)(2,1)S(1)}, u32[]{:S(2)}, u32[]{:S(2)}) async-start(bf16[16,16,4096]{2,1,0:T(8,128)(2,1)} %bitcast.39), calls=%async_computation.3 | async-start | bytes 4194304 | tf_op jit(solution)/shard_map/all_to_all | solution.py:22
  137.1 7.2 %copy-start.17 = (bf16[1024,2048]{1,0:T(8,128)(2,1)S(1)}, bf16[1024,2048]{1,0:T(8,128)(2,1)}, u32[]{:S(2)}) copy-start(bf16[1024,2048]{1,0:T(8,128)(2,1)} %param.10) | copy-start | bytes 12582916
  143.3 1.0 copy-start.8
  145.9 4.3 %copy-start.6 = (f32[256,1024]{1,0:T(8,128)}, f32[256,1024]{1,0:T(8,128)S(1)}, u32[]{:S(2)}) copy-start(f32[256,1024]{1,0:T(8,128)S(1)} %fusion.15) | copy-start | bytes 3145732
  164.1 34.5 %all-to-all-start.1 = ((bf16[16,16,4096]{2,1,0:T(8,128)(2,1)}), bf16[16,16,4096]{2,1,0:T(8,128)(2,1)}, u32[]{:S(2)}, u32[]{:S(2)}) async-start(bf16[16,16,4096]{2,1,0:T(8,128)(2,1)} %bitcast.38), calls=%async_computation.1 | async-start | bytes 4194304 | tf_op jit(solution)/shard_map/all_to_all | solution.py:22
  168.8 5.8 %copy-start.7 = (f32[256,1024]{1,0:T(8,128)S(1)}, f32[256,1024]{1,0:T(8,128)}, u32[]{:S(2)}) copy-start(f32[256,1024]{1,0:T(8,128)} %copy-done.6) | copy-start | bytes 3145732
  174.6 2.7 %copy-start.5 = (f32[256,1024]{1,0:T(8,128)S(1)}, f32[256,1024]{1,0:T(8,128)}, u32[]{:S(2)}) copy-start(f32[256,1024]{1,0:T(8,128)} %copy-done.4) | copy-start | bytes 3145732
  177.3 6.0 %copy-start.10 = (bf16[256,2048]{1,0:T(8,128)(2,1)S(1)}, bf16[256,2048]{1,0:T(8,128)(2,1)}, u32[]{:S(2)}) copy-start(bf16[256,2048]{1,0:T(8,128)(2,1)} %copy-done.9) | copy-start | bytes 3145732
  177.3 6.0 %copy-start.12 = (bf16[256,1024]{1,0:T(8,128)(2,1)S(1)}, bf16[256,1024]{1,0:T(8,128)(2,1)}, u32[]{:S(2)}) copy-start(bf16[256,1024]{1,0:T(8,128)(2,1)} %copy-done.11) | copy-start | bytes 1572868
  194.2 37.8 %collective-permute-start.4 = (bf16[128,2048]{1,0:T(8,128)(2,1)}, bf16[128,2048]{1,0:T(8,128)(2,1)}, u32[]{:S(2)}, u32[]{:S(2)}) collective-permute-start(bf16[128,2048]{1,0:T(8,128)(2,1)} %convolution_convert_fusion.8), channel_id=1, source_target_pairs={{0,4},{4,0},{1,5},{5,1},{2,6},{6,2},{3,7},{7,3},{8,12},{12,8},{9,1... | collective-permute-start | bytes 1572872 | tf_op jit(solution)/shard_map/ppermute | solution.py:33
  196.0 36.0 %copy-start = (bf16[128,2048]{1,0:T(8,128)(2,1)S(1)}, bf16[128,2048]{1,0:T(8,128)(2,1)}, u32[]{:S(2)}) copy-start(bf16[128,2048]{1,0:T(8,128)(2,1)} %param.7) | copy-start | bytes 1572868
  196.0 36.0 %copy-start.13 = (f32[2048]{0:T(1024)S(1)}, f32[2048]{0:T(1024)}, u32[]{:S(2)}) copy-start(f32[2048]{0:T(1024)} %param.8) | copy-start | bytes 24580
  197.2 46.1 %collective-permute-start.3 = (bf16[128,2048]{1,0:T(8,128)(2,1)}, bf16[128,2048]{1,0:T(8,128)(2,1)}, u32[]{:S(2)}, u32[]{:S(2)}) collective-permute-start(bf16[128,2048]{1,0:T(8,128)(2,1)} %add_convert_fusion.2), channel_id=1, source_target_pairs={{0,4},{4,0},{1,5},{5,1},{2,6},{6,2},{3,7},{7,3},{8,12},{12,8},{9,1... | collective-permute-start | bytes 1572872 | tf_op jit(solution)/shard_map/ppermute | solution.py:33
Sparse Core Ops, SparseCore 0:
  9.6 60.9 all-gather.1

commit v4 on v3

--- a/solution.py
+++ b/solution.py
@@ -127,15 +127,20 @@
         return mixed, dot(pick_rows, returned[:, features:], 0, 0)
 
     picks, pick_rows, arrived = send(blocks, weights, normed, out_cotangent)
+    far_normed, far_cot, arrived = lax.optimization_barrier((far_normed, far_cot, arrived))
     far_picks, far_pick_rows, far_arrived = send(far_blocks, far_weights, far_normed, far_cot)
     back, grads = look_up(arrived)
     far_back, far_grads = look_up(far_arrived)
     far_mixed, far_query = take(
         exchange(far_back, near_count), far_weights, far_picks, far_pick_rows
     )
-    mixed, query_sum = take(exchange(back, near_count), weights, picks, pick_rows)
-    other_query = across(far_query.astype(BF))
-    other_mixed = across(far_mixed.astype(BF))
+    far_query, far_mixed, back = lax.optimization_barrier(
+        (far_query.astype(BF), far_mixed.astype(BF), back)
+    )
+    other_query, other_mixed, returned = lax.optimization_barrier(
+        (across(far_query), across(far_mixed), exchange(back, near_count))
+    )
+    mixed, query_sum = take(returned, weights, picks, pick_rows)
     grad_values = (grads + far_grads).astype(BF)
 
     layer_out = exact_tokens + (mixed + other_mixed.astype(F32))

time: 254 us -> 255 us (level)
  waiting for transfers between devices: 127 us -> 119 us
  matrix products: 64.9 us -> 68.2 us
  local copies, waits for them, and re-layouts: 4.13 us -> 7.04 us
    all_to_all x4, waiting for transfers between devices: 49 us -> 42.2 us  [exchange(): lax.all_to_all(rows.reshape(owner_count, slots // owner_count, features),...]
    all_to_all x4, starting transfers between devices: 17.4 us -> 21.1 us  [exchange(): lax.all_to_all(rows.reshape(owner_count, slots // owner_count, features),...]
    dot_general x26, matrix products: 64.9 us -> 68.2 us  [dot(): lax.dot_general(left, right, (((left_dim,), (right_dim,)), ((), ())), pre...]
  transfers between devices with their start and end apart: 10 -> 10, of which waited for: 7 -> 8; matrix products, arithmetic and copies ran while one was open for 31% -> 22% of each run, Pallas kernels for 0% -> 0%
where the time goes in v4:
time: 255 us; the launch traced here: 254 us
  waiting for transfers between devices  119 us (47%)
  matrix products  68.2 us (27%)
  starting transfers between devices  29.7 us (12%)
  other arithmetic  15 us (6%)
  between operations  14.5 us (6%)
  local copies, waits for them, and re-layouts  7.04 us (3%)
    ppermute x5, waiting for transfers between devices, across(): return lax.ppermute(rows, 'half', [(0, 1), (1, 0)])  76.4 us
    dot_general x26, matrix products, dot(): lax.dot_general(left, right, (((left_dim,), (right_dim,)), ((), ())), pre...  68.2 us
    all_to_all x4, waiting for transfers between devices, exchange(): lax.all_to_all(rows.reshape(owner_count, slots // owner_count, features),...  42.2 us
    all_to_all x4, starting transfers between devices, exchange(): lax.all_to_all(rows.reshape(owner_count, slots // owner_count, features),...  21.1 us
    ppermute x5, starting transfers between devices, across(): return lax.ppermute(rows, 'half', [(0, 1), (1, 0)])  8.56 us
  transfers between devices with their start and end apart: 10, of which 8 were waited for; matrix products, arithmetic and copies ran while one was open for 22% of the time, Pallas kernels for 0%

profile of v4, /device:TPU:0, one launch (start us, length us, event | category | flops | bytes accessed | tf_op | source)
XLA Modules:
  0.0 253.7 jit_solution(5231943167958265109)
XLA Ops:
  7.2 0.7 all-gather.2.cloned.1.call-update
  7.9 0.7 broadcast_compare_fusion
  8.6 0.8 copy.38
  9.5 0.2 fusion.61
  9.8 0.2 fusion.23
  10.2 0.2 slice_reduce_fusion.6
  10.4 0.8 slice_bitcast_fusion
  11.3 0.2 slice_reduce_fusion.4
  11.7 1.2 fusion.32
  12.9 1.2 fusion.27
  14.2 0.8 copy-done.3
  15.0 0.4 convolution_convert_fusion.1
  15.4 0.4 fusion
  15.9 1.5 pad_maximum_fusion
  17.5 6.3 %all-to-all-start = ((bf16[16,16,4224]{2,1,0:T(8,128)(2,1)}), bf16[16,16,4224]{2,1,0:T(8,128)(2,1)S(1)}, u32[]{:S(2)}, u32[]{:S(2)}) async-start(bf16[16,16,4224]{2,1,0:T(8,128)(2,1)} %bitcast.2), calls=%async_computation | async-start | bytes 4325376 | tf_op jit(solution)/shard_map/all_to_all | solution.py:22
  23.9 2.6 %collective-permute-start = (f32[128,4]{1,0:T(8,128)S(1)}, f32[128,4]{1,0:T(8,128)S(1)}, u32[]{:S(2)}, u32[]{:S(2)}) collective-permute-start(f32[128,4]{1,0:T(8,128)S(1)} %copy.45), channel_id=1, source_target_pairs={{0,4},{4,0},{1,5},{5,1},{2,6},{6,2},{3,7},{7,3},{8,12},{12,8},{9,1... | collective-permute-start | bytes 6152 | tf_op jit(solution)/shard_map/ppermute | solution.py:33
  26.6 0.3 collective-permute-start.1
  26.9 2.6 %collective-permute-start.2 = (bf16[128,2048]{1,0:T(8,128)(2,1)S(1)}, bf16[128,2048]{1,0:T(8,128)(2,1)}, u32[]{:S(2)}, u32[]{:S(2)}) collective-permute-start(bf16[128,2048]{1,0:T(8,128)(2,1)S(1)} %copy-done.2), channel_id=1, source_target_pairs={{0,4},{4,0},{1,5},{5,1},{2,6},{6,2},{3,7},{7,3},{8,12},{12,8},{9,1... | collective-permute-start | bytes 1572872 | tf_op jit(solution)/shard_map/ppermute | solution.py:33
  29.5 20.3 %collective-permute-done = f32[128,4]{1,0:T(8,128)S(1)} collective-permute-done((f32[128,4]{1,0:T(8,128)S(1)}, f32[128,4]{1,0:T(8,128)S(1)}, u32[]{:S(2)}, u32[]{:S(2)}) %collective-permute-start) | collective-permute-done | bytes 2080 | tf_op jit(solution)/shard_map/ppermute | solution.py:33
  50.1 0.2 fusion.24
  50.7 0.2 slice_reduce_fusion.2
  51.5 9.6 %collective-permute-done.1 = bf16[128,2048]{1,0:T(8,128)(2,1)} collective-permute-done((bf16[128,2048]{1,0:T(8,128)(2,1)}, bf16[128,2048]{1,0:T(8,128)(2,1)}, u32[]{:S(2)}, u32[]{:S(2)}) %collective-permute-start.1) | collective-permute-done | bytes 524320 | tf_op jit(solution)/shard_map/ppermute | solution.py:33
  61.1 10.9 %collective-permute-done.2 = bf16[128,2048]{1,0:T(8,128)(2,1)} collective-permute-done((bf16[128,2048]{1,0:T(8,128)(2,1)S(1)}, bf16[128,2048]{1,0:T(8,128)(2,1)}, u32[]{:S(2)}, u32[]{:S(2)}) %collective-permute-start.2) | collective-permute-done | bytes 524320 | tf_op jit(solution)/shard_map/ppermute | solution.py:33
  72.0 2.4 all-to-all-done
  74.5 1.8 convolution_convert_fusion
  76.3 1.5 fusion.1
  77.9 1.5 pad_maximum_fusion.1
  79.4 6.4 %all-to-all-start.1 = ((bf16[16,16,4224]{2,1,0:T(8,128)(2,1)}), bf16[16,16,4224]{2,1,0:T(8,128)(2,1)}, u32[]{:S(2)}, u32[]{:S(2)}) async-start(bf16[16,16,4224]{2,1,0:T(8,128)(2,1)} %bitcast.4), calls=%async_computation.1 | async-start | bytes 4325376 | tf_op jit(solution)/shard_map/all_to_all | solution.py:22
  85.8 28.7 %all-to-all-done.1 = bf16[16,16,4224]{2,1,0:T(8,128)(2,1)} async-done(((bf16[16,16,4224]{2,1,0:T(8,128)(2,1)}), bf16[16,16,4224]{2,1,0:T(8,128)(2,1)}, u32[]{:S(2)}, u32[]{:S(2)}) %all-to-all-start.1) | async-done | bytes 2162720 | tf_op jit(solution)/shard_map/all_to_all | solution.py:22
  114.6 1.0 add_reduce_fusion.1
  115.6 6.2 %convolution_convert_fusion.7 = bf16[256,2048]{1,0:T(8,128)(2,1)S(1)} fusion(bf16[2048,2048]{1,0:T(8,128)(2,1)} %all-gather.2.cloned.1.call-done, bf16[256,4224]{1,0:T(8,128)(2,1)} %bitcast.5), kind=kOutput, calls=%fused_computation.12 | convolution fusion | flops 2148007936 | bytes 10485760 | tf_op jit(solution)/shard_map/dot_general | solution.py:15
  121.8 1.0 copy-done.8
  122.7 1.5 fusion.18
  124.2 3.0 %fusion.21 = bf16[256,1024]{1,0:T(8,128)(2,1)S(1)} fusion(f32[256,1024]{1,0:T(8,128)S(1)} %fusion.18, bf16[1024,2048]{1,0:T(8,128)(2,1)S(1)} %copy-done.17, bf16[256,4224]{1,0:T(8,128)(2,1)} %bitcast.5, s32[1024]{0:T(1024)S(1)} %add_select_fusion.12, s32[256]{0:T(256)S(1)} %add_reduce_fusion.1), kind=kOutput, calls=%fused_computation.51 | convolution fusion | flops 1075576832 | bytes 6820864 | tf_op jit(solution)/shard_map/dot_general | solution.py:15
  127.3 1.3 convolution_convert_fusion.5
  128.6 1.3 convolution_convert_fusion.4
  129.9 1.5 pad_maximum_fusion.2
  131.4 4.4 %all-to-all-start.2 = ((bf16[16,16,4096]{2,1,0:T(8,128)(2,1)}), bf16[16,16,4096]{2,1,0:T(8,128)(2,1)S(1)}, u32[]{:S(2)}, u32[]{:S(2)}) async-start(bf16[16,16,4096]{2,1,0:T(8,128)(2,1)} %bitcast.42), calls=%async_computation.2 | async-start | bytes 4194304 | tf_op jit(solution)/shard_map/all_to_all | solution.py:22
  135.8 1.0 add_reduce_fusion
  136.8 6.2 %convolution_convert_fusion.6 = bf16[256,2048]{1,0:T(8,128)(2,1)S(1)} fusion(bf16[2048,2048]{1,0:T(8,128)(2,1)} %all-gather.2.cloned.1.call-done, bf16[256,4224]{1,0:T(8,128)(2,1)} %bitcast.44), kind=kOutput, calls=%fused_computation.11 | convolution fusion | flops 2148007936 | bytes 10485760 | tf_op jit(solution)/shard_map/dot_general | solution.py:15
  143.0 1.0 copy-done.9
  143.9 1.5 fusion.20
  145.5 3.0 %fusion.22 = bf16[256,1024]{1,0:T(8,128)(2,1)S(1)} fusion(f32[256,1024]{1,0:T(8,128)S(1)} %fusion.20, bf16[1024,2048]{1,0:T(8,128)(2,1)S(1)} %copy-done.18, bf16[256,4224]{1,0:T(8,128)(2,1)} %bitcast.45, s32[1024]{0:T(1024)S(1)} %add_select_fusion.12, s32[256]{0:T(256)S(1)} %add_reduce_fusion), kind=kOutput, calls=%fused_computation.52 | convolution fusion | flops 1075576832 | bytes 6820864 | tf_op jit(solution)/shard_map/dot_general | solution.py:15
  148.5 1.3 convolution_convert_fusion.2
  149.8 1.3 convolution_convert_fusion.3
  151.1 1.5 pad_maximum_fusion.3
  152.7 11.0 %all-to-all-done.2 = bf16[16,16,4096]{2,1,0:T(8,128)(2,1)S(1)} async-done(((bf16[16,16,4096]{2,1,0:T(8,128)(2,1)}), bf16[16,16,4096]{2,1,0:T(8,128)(2,1)S(1)}, u32[]{:S(2)}, u32[]{:S(2)}) %all-to-all-start.2) | async-done | bytes 2097184 | tf_op jit(solution)/shard_map/all_to_all | solution.py:22
  163.7 1.2 convolution_convert_fusion.8
  164.8 0.3 fusion.41
  165.2 1.2 add_convert_fusion.1
  166.3 4.0 %all-to-all-start.3 = ((bf16[16,16,4096]{2,1,0:T(8,128)(2,1)}), bf16[16,16,4096]{2,1,0:T(8,128)(2,1)S(1)}, u32[]{:S(2)}, u32[]{:S(2)}) async-start(bf16[16,16,4096]{2,1,0:T(8,128)(2,1)} %bitcast.41), calls=%async_computation.3 | async-start | bytes 4194304 | tf_op jit(solution)/shard_map/all_to_all | solution.py:22
  170.4 5.8 %fusion.125 = f32[1024,2048]{1,0:T(8,128)} fusion(bf16[256,1024]{1,0:T(8,128)(2,1)S(1)} %fusion.21, bf16[256,2048]{1,0:T(8,128)(2,1)} %copy-done.8), kind=kOutput, calls=%fused_computation.215 | convolution fusion | flops 1073741824 | bytes 9961472 | tf_op jit(solution)/shard_map/dot_general | solution.py:15
  176.2 4.5 %fusion.124 = f32[1024,2048]{1,0:T(8,128)} fusion(bf16[256,1024]{1,0:T(8,128)(2,1)S(1)} %copy-done.13, bf16[256,2048]{1,0:T(8,128)(2,1)S(1)} %copy-done.10), kind=kOutput, calls=%fused_computation.214 | convolution fusion | flops 1073741824 | bytes 9961472 | tf_op jit(solution)/shard_map/dot_general | solution.py:15
  180.8 2.7 %fusion.43 = f32[1024,2048]{1,0:T(8,128)S(1)} fusion(bf16[256,4224]{1,0:T(8,128)(2,1)} %bitcast.5, f32[256,1024]{1,0:T(8,128)S(1)} %copy-done.5, s32[1024]{0:T(1024)S(1)} %add_select_fusion.12, s32[256]{0:T(256)S(1)} %add_reduce_fusion.1), kind=kOutput, calls=%fused_computation.75 | convolution fusion | flops 1074266112 | bytes 10490880 | tf_op jit(solution)/shard_map/dot_general | solution.py:15
  183.5 2.4 collective-permute-start.3
  185.9 0.5 collective-permute-start.4
  186.5 9.6 %add_convert_fusion = bf16[1024,2048]{1,0:T(8,128)(2,1)} fusion(f32[1024,2048]{1,0:T(8,128)S(1)} %fusion.43, f32[1024,2048]{1,0:T(8,128)} %fusion.125, f32[1024,2048]{1,0:T(8,128)} %fusion.124, bf16[256,4224]{1,0:T(8,128)(2,1)} %bitcast.46, f32[256,1024]{1,0:T(8,128)S(1)} %copy-done.7, s32[1024]{0:T(1024)S(1)} %add_select_fusion.12, s32[256]{0:T(256)S(1)} %add_reduce_fusion), kind=kOutput, calls=%fused_computation | convolution fusion | flops 1082654720 | bytes 31462400 | tf_op jit(solution)/shard_map/dot_general | solution.py:15
  196.1 10.2 %collective-permute-done.3 = bf16[128,2048]{1,0:T(8,128)(2,1)S(1)} collective-permute-done((bf16[128,2048]{1,0:T(8,128)(2,1)}, bf16[128,2048]{1,0:T(8,128)(2,1)S(1)}, u32[]{:S(2)}, u32[]{:S(2)}) %collective-permute-start.3) | collective-permute-done | bytes 524320 | tf_op jit(solution)/shard_map/ppermute | solution.py:33
  206.2 0.8 copy-done.11
  207.0 25.5 %collective-permute-done.4 = bf16[128,2048]{1,0:T(8,128)(2,1)} collective-permute-done((bf16[128,2048]{1,0:T(8,128)(2,1)}, bf16[128,2048]{1,0:T(8,128)(2,1)}, u32[]{:S(2)}, u32[]{:S(2)}) %collective-permute-start.4) | collective-permute-done | bytes 524320 | tf_op jit(solution)/shard_map/ppermute | solution.py:33
  232.5 1.3 convolution_multiply_fusion.4
  233.8 7.7 %fusion.28 = (f32[128]{0:T(128)S(1)}, f32[128,2048]{1,0:T(8,128)}) fusion(bf16[128,2048]{1,0:T(8,128)(2,1)S(1)} %copy-done, f32[128]{0:T(128)S(1)} %add_rsqrt_fusion, f32[2048]{0:T(1024)S(1)} %copy-done.14, bf16[2048,2048]{1,0:T(8,128)(2,1)} %all-gather.2.cloned.1.call-done, bf16[128,2048]{1,0:T(8,128)(2,1)} %copy-done.11, ...), kind=kOutput, calls=%fused_computation.60 | convolution fusion | flops 1210318720 | bytes 11544576 | tf_op jit(solution)/shard_map/dot_general | solution.py:15
  241.5 2.6 %fusion.31 = f32[128,2048]{1,0:T(8,128)} fusion(f32[128,2048]{1,0:T(8,128)} %get-tuple-element.38, bf16[128,2048]{1,0:T(8,128)(2,1)S(1)} %copy-done, bf16[128,2048]{1,0:T(8,128)(2,1)S(1)} %copy-done.2, f32[128]{0:T(128)S(1)} %broadcast_multiply_fusion, f32[128]{0:T(128)S(1)} %add_rsqrt_fusion), kind=kLoop, calls=%fused_computation.63 | loop fusion | flops 1835008 | bytes 3146752 | tf_op jit(solution)/shard_map/add | solution.py:149
  244.1 2.8 %fusion.4 = f32[128,2048]{1,0:T(8,128)} fusion(f32[128,2048]{1,0:T(8,128)} %convolution_multiply_fusion.4, bf16[128,2048]{1,0:T(8,128)(2,1)S(1)} %copy-done, bf16[128,2048]{1,0:T(8,128)(2,1)} %collective-permute-done.4, bf16[256,4096]{1,0:T(8,128)(2,1)S(1)} %bitcast.40, f32[128]{0:T(128)S(1)} %get-tuple-element.35, s32[128]{0:T(128)S(1)} %get-tuple-element.23), kind=kOutput, calls=%fused_computation.18 | convolution fusion | flops 135823360 | bytes 4195328 | tf_op jit(solution)/shard_map/dot_general | solution.py:15
  (67 shorter events, 2.6 us)
Async XLA Ops:
  7.2 8.2 %copy-start.2 = (bf16[128,2048]{1,0:T(8,128)(2,1)S(1)}, bf16[128,2048]{1,0:T(8,128)(2,1)}, u32[]{:S(2)}) copy-start(bf16[128,2048]{1,0:T(8,128)(2,1)} %param.13) | copy-start | bytes 1572868
  7.2 108.4 %all-gather.2.cloned.1.call-start = ((), (), s32[]{:S(2)}) async-start(), calls=%async_computation.4 | async-start | bytes 10485760 | tf_op jit(solution)/shard_map/all_gather | solution.py:75
  14.2 0.8 copy-start.3
  15.9 7.8 %copy-start.15 = (s32[128,2]{0,1:T(2,128)S(1)}, s32[128,2]{0,1:T(2,128)}, u32[]{:S(2)}) copy-start(s32[128,2]{0,1:T(2,128)} %param.11) | copy-start | bytes 3076
  15.9 7.8 %copy-start.16 = (f32[128,2]{0,1:T(2,128)S(1)}, f32[128,2]{0,1:T(2,128)}, u32[]{:S(2)}) copy-start(f32[128,2]{0,1:T(2,128)} %param.12) | copy-start | bytes 3076
  17.5 57.0 %all-to-all-start = ((bf16[16,16,4224]{2,1,0:T(8,128)(2,1)}), bf16[16,16,4224]{2,1,0:T(8,128)(2,1)S(1)}, u32[]{:S(2)}, u32[]{:S(2)}) async-start(bf16[16,16,4224]{2,1,0:T(8,128)(2,1)} %bitcast.2), calls=%async_computation | async-start | bytes 4325376 | tf_op jit(solution)/shard_map/all_to_all | solution.py:22
  23.9 25.8 %collective-permute-start = (f32[128,4]{1,0:T(8,128)S(1)}, f32[128,4]{1,0:T(8,128)S(1)}, u32[]{:S(2)}, u32[]{:S(2)}) collective-permute-start(f32[128,4]{1,0:T(8,128)S(1)} %copy.45), channel_id=1, source_target_pairs={{0,4},{4,0},{1,5},{5,1},{2,6},{6,2},{3,7},{7,3},{8,12},{12,8},{9,1... | collective-permute-start | bytes 6152 | tf_op jit(solution)/shard_map/ppermute | solution.py:33
  26.6 34.5 %collective-permute-start.1 = (bf16[128,2048]{1,0:T(8,128)(2,1)}, bf16[128,2048]{1,0:T(8,128)(2,1)}, u32[]{:S(2)}, u32[]{:S(2)}) collective-permute-start(bf16[128,2048]{1,0:T(8,128)(2,1)} %copy-done.3), channel_id=1, source_target_pairs={{0,4},{4,0},{1,5},{5,1},{2,6},{6,2},{3,7},{7,3},{8,12},{12,8},{9,1... | collective-permute-start | bytes 1572872 | tf_op jit(solution)/shard_map/ppermute | solution.py:33
  26.9 45.1 %collective-permute-start.2 = (bf16[128,2048]{1,0:T(8,128)(2,1)S(1)}, bf16[128,2048]{1,0:T(8,128)(2,1)}, u32[]{:S(2)}, u32[]{:S(2)}) collective-permute-start(bf16[128,2048]{1,0:T(8,128)(2,1)S(1)} %copy-done.2), channel_id=1, source_target_pairs={{0,4},{4,0},{1,5},{5,1},{2,6},{6,2},{3,7},{7,3},{8,12},{12,8},{9,1... | collective-permute-start | bytes 1572872 | tf_op jit(solution)/shard_map/ppermute | solution.py:33
  74.5 4.9 %copy-start.1 = (bf16[16,16,4224]{2,1,0:T(8,128)(2,1)}, bf16[16,16,4224]{2,1,0:T(8,128)(2,1)S(1)}, u32[]{:S(2)}) copy-start(bf16[16,16,4224]{2,1,0:T(8,128)(2,1)S(1)} %all-to-all-done) | copy-start | bytes 6488068
  79.4 35.2 %all-to-all-start.1 = ((bf16[16,16,4224]{2,1,0:T(8,128)(2,1)}), bf16[16,16,4224]{2,1,0:T(8,128)(2,1)}, u32[]{:S(2)}, u32[]{:S(2)}) async-start(bf16[16,16,4224]{2,1,0:T(8,128)(2,1)} %bitcast.4), calls=%async_computation.1 | async-start | bytes 4325376 | tf_op jit(solution)/shard_map/all_to_all | solution.py:22
  115.6 7.2 %copy-start.17 = (bf16[1024,2048]{1,0:T(8,128)(2,1)S(1)}, bf16[1024,2048]{1,0:T(8,128)(2,1)}, u32[]{:S(2)}) copy-start(bf16[1024,2048]{1,0:T(8,128)(2,1)} %param.10) | copy-start | bytes 12582916
  121.8 1.0 copy-start.8
  124.2 3.1 %copy-start.4 = (f32[256,1024]{1,0:T(8,128)}, f32[256,1024]{1,0:T(8,128)S(1)}, u32[]{:S(2)}) copy-start(f32[256,1024]{1,0:T(8,128)S(1)} %fusion.18) | copy-start | bytes 3145732
  131.4 32.3 %all-to-all-start.2 = ((bf16[16,16,4096]{2,1,0:T(8,128)(2,1)}), bf16[16,16,4096]{2,1,0:T(8,128)(2,1)S(1)}, u32[]{:S(2)}, u32[]{:S(2)}) async-start(bf16[16,16,4096]{2,1,0:T(8,128)(2,1)} %bitcast.42), calls=%async_computation.2 | async-start | bytes 4194304 | tf_op jit(solution)/shard_map/all_to_all | solution.py:22
  136.7 7.2 %copy-start.18 = (bf16[1024,2048]{1,0:T(8,128)(2,1)S(1)}, bf16[1024,2048]{1,0:T(8,128)(2,1)}, u32[]{:S(2)}) copy-start(bf16[1024,2048]{1,0:T(8,128)(2,1)} %param.10) | copy-start | bytes 12582916
  142.9 1.0 copy-start.9
  145.4 4.3 %copy-start.6 = (f32[256,1024]{1,0:T(8,128)}, f32[256,1024]{1,0:T(8,128)S(1)}, u32[]{:S(2)}) copy-start(f32[256,1024]{1,0:T(8,128)S(1)} %fusion.20) | copy-start | bytes 3145732
  148.5 2.6 %copy-start.12 = (bf16[256,1024]{1,0:T(8,128)(2,1)}, bf16[256,1024]{1,0:T(8,128)(2,1)S(1)}, u32[]{:S(2)}) copy-start(bf16[256,1024]{1,0:T(8,128)(2,1)S(1)} %fusion.22) | copy-start | bytes 1572868
  166.3 66.1 %all-to-all-start.3 = ((bf16[16,16,4096]{2,1,0:T(8,128)(2,1)}), bf16[16,16,4096]{2,1,0:T(8,128)(2,1)S(1)}, u32[]{:S(2)}, u32[]{:S(2)}) async-start(bf16[16,16,4096]{2,1,0:T(8,128)(2,1)} %bitcast.41), calls=%async_computation.3 | async-start | bytes 4194304 | tf_op jit(solution)/shard_map/all_to_all | solution.py:22
  170.4 5.9 %copy-start.10 = (bf16[256,2048]{1,0:T(8,128)(2,1)S(1)}, bf16[256,2048]{1,0:T(8,128)(2,1)}, u32[]{:S(2)}) copy-start(bf16[256,2048]{1,0:T(8,128)(2,1)} %copy-done.9) | copy-start | bytes 3145732
  170.4 5.9 %copy-start.13 = (bf16[256,1024]{1,0:T(8,128)(2,1)S(1)}, bf16[256,1024]{1,0:T(8,128)(2,1)}, u32[]{:S(2)}) copy-start(bf16[256,1024]{1,0:T(8,128)(2,1)} %copy-done.12) | copy-start | bytes 1572868
  176.2 4.5 %copy-start.5 = (f32[256,1024]{1,0:T(8,128)S(1)}, f32[256,1024]{1,0:T(8,128)}, u32[]{:S(2)}) copy-start(f32[256,1024]{1,0:T(8,128)} %copy-done.4) | copy-start | bytes 3145732
  180.8 5.7 %copy-start.7 = (f32[256,1024]{1,0:T(8,128)S(1)}, f32[256,1024]{1,0:T(8,128)}, u32[]{:S(2)}) copy-start(f32[256,1024]{1,0:T(8,128)} %copy-done.6) | copy-start | bytes 3145732
  183.4 50.4 %copy-start = (bf16[128,2048]{1,0:T(8,128)(2,1)S(1)}, bf16[128,2048]{1,0:T(8,128)(2,1)}, u32[]{:S(2)}) copy-start(bf16[128,2048]{1,0:T(8,128)(2,1)} %param.7) | copy-start | bytes 1572868
  183.5 50.4 %copy-start.14 = (f32[2048]{0:T(1024)S(1)}, f32[2048]{0:T(1024)}, u32[]{:S(2)}) copy-start(f32[2048]{0:T(1024)} %param.8) | copy-start | bytes 24580
  183.5 22.8 %collective-permute-start.3 = (bf16[128,2048]{1,0:T(8,128)(2,1)}, bf16[128,2048]{1,0:T(8,128)(2,1)S(1)}, u32[]{:S(2)}, u32[]{:S(2)}) collective-permute-start(bf16[128,2048]{1,0:T(8,128)(2,1)} %convolution_convert_fusion.8), channel_id=1, source_target_pairs={{0,4},{4,0},{1,5},{5,1},{2,6},{6,2},{3,7},{7,3},{8,12},{12,8},{9,1... | collective-permute-start | bytes 1572872 | tf_op jit(solution)/shard_map/ppermute | solution.py:33
  185.9 46.6 %collective-permute-start.4 = (bf16[128,2048]{1,0:T(8,128)(2,1)}, bf16[128,2048]{1,0:T(8,128)(2,1)}, u32[]{:S(2)}, u32[]{:S(2)}) collective-permute-start(bf16[128,2048]{1,0:T(8,128)(2,1)} %add_convert_fusion.1), channel_id=1, source_target_pairs={{0,4},{4,0},{1,5},{5,1},{2,6},{6,2},{3,7},{7,3},{8,12},{12,8},{9,1... | collective-permute-start | bytes 1572872 | tf_op jit(solution)/shard_map/ppermute | solution.py:33
  206.2 0.8 copy-start.11
Sparse Core Ops, SparseCore 0:
  9.6 93.0 all-gather.1

commit v5 on v2

--- a/solution.py
+++ b/solution.py
@@ -90,12 +90,17 @@
     scores = dot(query_rows, values, 1, 1) * score_scale
     sigmoid_of = jax.nn.sigmoid(scores)
     gate_values = jnp.where(in_block, sigmoid_of, 0.0).astype(BF)
-    parts_back = exchange(dot(gate_values, values).astype(BF), owner_count)
     cot_scores = dot(cot_rows, values, 1, 1)
     score_grads = jnp.where(
         in_block, cot_scores * sigmoid_of * (1.0 - sigmoid_of) * score_scale, 0.0
     ).astype(BF)
-    grads_back = exchange(dot(score_grads, values).astype(BF), owner_count)
+    back = exchange(
+        jnp.concatenate(
+            [dot(gate_values, values).astype(BF), dot(score_grads, values).astype(BF)], axis=1
+        ),
+        owner_count,
+    )
+    parts_back, grads_back = back[:, :features], back[:, features:]
     grad_values = (dot(gate_values, cot_rows, 0, 0) + dot(score_grads, query_rows, 0, 0)).astype(BF)
 
     mixed = sum(

time: 257 us -> 263 us (1.023)
  waiting for transfers between devices: 162 us -> 171 us
  matrix products: 51.8 us -> 47.5 us
    all_to_all x4 -> x3, waiting for transfers between devices: 128 us -> 137 us  [exchange(): lax.all_to_all(rows.reshape(owner_count, slots // owner_count, features),...]
    dot_general x13, matrix products: 51.8 us -> 47.5 us  [dot(): lax.dot_general(left, right, (((left_dim,), (right_dim,)), ((), ())), pre...]
    all_to_all x4 -> x3, starting transfers between devices: 18.3 us -> 17.3 us  [exchange(): lax.all_to_all(rows.reshape(owner_count, slots // owner_count, features),...]
  transfers between devices with their start and end apart: 5 -> 4, of which waited for: 5 -> 3; matrix products, arithmetic and copies ran while one was open for 17% -> 12% of each run, Pallas kernels for 0% -> 0%
where the time goes in v5:
time: 263 us; the launch traced here: 262 us
  waiting for transfers between devices  171 us (65%)
  matrix products  47.5 us (18%)
  starting transfers between devices  17.4 us (7%)
  between operations  14.3 us (5%)
  other arithmetic  7.16 us (3%)
  local copies, waits for them, and re-layouts  4.71 us (2%)
    all_to_all x3, waiting for transfers between devices, exchange(): lax.all_to_all(rows.reshape(owner_count, slots // owner_count, features),...  137 us
    dot_general x13, matrix products, dot(): lax.dot_general(left, right, (((left_dim,), (right_dim,)), ((), ())), pre...  47.5 us
    all_gather x1, waiting for transfers between devices, body(): weight_full = lax.all_gather(query_weight, 'dp', axis=1, tiled=True)  33.2 us
    all_to_all x3, starting transfers between devices, exchange(): lax.all_to_all(rows.reshape(owner_count, slots // owner_count, features),...  17.3 us
  transfers between devices with their start and end apart: 4, of which 3 were waited for; matrix products, arithmetic and copies ran while one was open for 12% of the time, Pallas kernels for 0%

profile of v5, /device:TPU:0, one launch (start us, length us, event | category | flops | bytes accessed | tf_op | source)
XLA Modules:
  0.0 262.4 jit_solution(7648111344957566032)
XLA Ops:
  7.2 0.0 copy-start.6
  7.2 0.0 copy-start
  7.2 0.0 copy-start.5
  7.2 0.0 all-gather.2.cloned.1.call-start
  7.2 0.7 all-gather.2.cloned.1.call-update
  7.9 0.0 copy-done.6
  7.9 0.1 copy.27
  8.1 0.1 copy.32
  8.2 0.1 reshape.104
  8.4 0.2 fusion.11
  8.6 0.1 convert_element_type.66
  8.7 0.1 fusion.42
  8.8 0.2 slice_reduce_fusion
  9.0 0.2 slice_reduce_fusion.2
  9.2 0.2 select_reduce_fusion
  9.4 0.0 copy-done
  9.4 0.2 fusion.19
  9.6 0.0 copy-done.5
  9.6 0.8 convolution_convert_fusion.2
  10.4 0.1 broadcast_in_dim.81
  10.6 1.6 pad_maximum_fusion.1
  12.1 0.0 copy-start.7
  12.1 0.0 copy-start.4
  12.1 7.3 %all-to-all-start = ((bf16[32,16,2176]{2,1,0:T(8,128)(2,1)}), bf16[32,16,2176]{2,1,0:T(8,128)(2,1)S(1)}, u32[]{:S(2)}, u32[]{:S(2)}) async-start(bf16[32,16,2176]{2,1,0:T(8,128)(2,1)} %bitcast.2), calls=%async_computation | async-start | bytes 4456448 | tf_op jit(solution)/shard_map/all_to_all | solution.py:21
  19.4 0.0 copy-done.7
  19.4 0.2 select_reduce_fusion.2
  19.7 0.0 copy-done.4
  19.7 2.1 multiply_convert_fusion
  21.8 50.6 %all-to-all-done = bf16[32,16,2176]{2,1,0:T(8,128)(2,1)S(1)} async-done(((bf16[32,16,2176]{2,1,0:T(8,128)(2,1)}), bf16[32,16,2176]{2,1,0:T(8,128)(2,1)S(1)}, u32[]{:S(2)}, u32[]{:S(2)}) %all-to-all-start) | async-done | bytes 2228256 | tf_op jit(solution)/shard_map/all_to_all | solution.py:21
  72.4 0.0 copy-start.1
  72.4 1.4 copy-done.1
  73.8 2.9 %all-to-all-start.1 = ((bf16[32,16,2048]{2,1,0:T(8,128)(2,1)}), bf16[32,16,2048]{2,1,0:T(8,128)(2,1)S(1)}, u32[]{:S(2)}, u32[]{:S(2)}) async-start(bf16[32,16,2048]{2,1,0:T(8,128)(2,1)} %bitcast.4), calls=%async_computation.1 | async-start | bytes 4194304 | tf_op jit(solution)/shard_map/all_to_all | solution.py:21
  76.7 1.1 add_reduce_fusion
  77.8 33.2 %all-gather.2.cloned.1.call-done = bf16[2048,2048]{1,0:T(8,128)(2,1)} async-done(((bf16[2048,512]{1,0:T(8,128)(2,1)}), bf16[2048,2048]{1,0:T(8,128)(2,1)}) %all-gather.2.cloned.1.call-update) | async-done | bytes 8388624 | tf_op jit(solution)/shard_map/all_gather | solution.py:41
  111.0 0.0 copy-start.8
  111.0 8.7 %convolution_convert_fusion.3 = bf16[512,2048]{1,0:T(8,128)(2,1)S(1)} fusion(bf16[2048,2048]{1,0:T(8,128)(2,1)} %all-gather.2.cloned.1.call-done, bf16[512,2176]{1,0:T(8,128)(2,1)} %bitcast.27), kind=kOutput, calls=%fused_computation.6 | convolution fusion | flops 4296015872 | bytes 12582912 | tf_op jit(solution)/shard_map/dot_general | solution.py:14
  119.7 0.0 copy-done.8
  119.7 0.0 copy-start.10
  119.7 2.6 add_divide_fusion
  122.3 0.0 copy-done.10
  122.3 0.0 copy-start.2
  122.3 1.3 copy-done.2
  123.6 3.7 %convolution_convert_fusion.1 = bf16[512,2048]{1,0:T(8,128)(2,1)} fusion(bf16[1024,2048]{1,0:T(8,128)(2,1)S(1)} %copy-done.8, f32[512,1024]{1,0:T(8,128)S(1)} %add_divide_fusion, s32[1024]{0:T(1024)S(1)} %add_select_fusion.2, s32[512]{0:T(512)S(1)} %add_reduce_fusion), kind=kOutput, calls=%fused_computation.4 | convolution fusion | flops 2149580800 | bytes 8394752 | tf_op jit(solution)/shard_map/dot_general | solution.py:14
  127.4 0.0 all-to-all-done.1
  127.4 0.0 copy-start.9
  127.4 5.6 %fusion.3 = bf16[512,1024]{1,0:T(8,128)(2,1)S(1)} fusion(f32[512,1024]{1,0:T(8,128)} %copy-done.2, bf16[512,2048]{1,0:T(8,128)(2,1)S(1)} %bitcast.24, bf16[1024,2048]{1,0:T(8,128)(2,1)} %param.10, s32[1024]{0:T(1024)S(1)} %add_select_fusion.2, s32[512]{0:T(512)S(1)} %add_reduce_fusion), kind=kOutput, calls=%fused_computation.17 | convolution fusion | flops 2151153664 | bytes 9443328 | tf_op jit(solution)/shard_map/dot_general | solution.py:14
  133.0 0.0 copy-start.12
  133.0 1.0 copy-done.12
  133.9 0.0 copy-done.9
  133.9 2.4 convolution_convert_fusion
  136.3 0.0 copy-done.3
  136.3 2.5 pad_maximum_fusion
  138.8 7.1 %all-to-all-start.2 = ((bf16[32,16,4096]{2,1,0:T(8,128)(2,1)}), bf16[32,16,4096]{2,1,0:T(8,128)(2,1)}, u32[]{:S(2)}, u32[]{:S(2)}) async-start(bf16[32,16,4096]{2,1,0:T(8,128)(2,1)} %bitcast.23), calls=%async_computation.2 | async-start | bytes 8388608 | tf_op jit(solution)/shard_map/all_to_all | solution.py:21
  145.9 0.0 copy-start.11
  145.9 0.0 copy-start.13
  145.9 4.3 %fusion.49 = f32[1024,2048]{1,0:T(8,128)S(1)} fusion(bf16[512,2048]{1,0:T(8,128)(2,1)S(1)} %bitcast.25, f32[512,1024]{1,0:T(8,128)} %copy-done.2, s32[1024]{0:T(1024)S(1)} %add_select_fusion.2, s32[512]{0:T(512)S(1)} %add_reduce_fusion), kind=kOutput, calls=%fused_computation.91 | convolution fusion | flops 2148532224 | bytes 12589056 | tf_op jit(solution)/shard_map/dot_general | solution.py:14
  150.2 0.0 copy-done.11
  150.2 0.0 copy-done.13
  150.2 4.7 %add_convert_fusion = bf16[1024,2048]{1,0:T(8,128)(2,1)} fusion(f32[1024,2048]{1,0:T(8,128)S(1)} %fusion.49, bf16[512,1024]{1,0:T(8,128)(2,1)S(1)} %copy-done.13, bf16[512,2048]{1,0:T(8,128)(2,1)S(1)} %copy-done.11), kind=kOutput, calls=%fused_computation | convolution fusion | flops 2151677952 | bytes 15728640 | tf_op jit(solution)/shard_map/dot_general | solution.py:14
  154.8 86.8 %all-to-all-done.2 = bf16[32,16,4096]{2,1,0:T(8,128)(2,1)} async-done(((bf16[32,16,4096]{2,1,0:T(8,128)(2,1)}), bf16[32,16,4096]{2,1,0:T(8,128)(2,1)}, u32[]{:S(2)}, u32[]{:S(2)}) %all-to-all-start.2) | async-done | bytes 4194336 | tf_op jit(solution)/shard_map/all_to_all | solution.py:21
  241.6 2.1 convolution_multiply_fusion.2
  243.7 7.4 %fusion.15 = (f32[128]{0:T(128)S(1)}, f32[128,2048]{1,0:T(8,128)S(1)}) fusion(bf16[128,2048]{1,0:T(8,128)(2,1)S(1)} %copy-done, f32[128]{0:T(128)S(1)} %add_rsqrt_fusion, f32[2048]{0:T(1024)S(1)} %copy-done.5, bf16[2048,2048]{1,0:T(8,128)(2,1)} %all-gather.2.cloned.1.call-done, bf16[512,4096]{1,0:T(8,128)(2,1)} %bitcast.7, s32[128]{0:T(128)S(1)} %get-tuple-element.9, ...), kind=kOutput, calls=%fused_computation.31 | convolution fusion | flops 1344274304 | bytes 12068864 | tf_op jit(solution)/shard_map/dot_general | solution.py:14
  251.1 3.1 %fusion.1 = f32[128,2048]{1,0:T(8,128)} fusion(f32[128,2048]{1,0:T(8,128)S(1)} %convolution_multiply_fusion.2, bf16[512,4096]{1,0:T(8,128)(2,1)} %bitcast.7, bf16[128,2048]{1,0:T(8,128)(2,1)S(1)} %copy-done, f32[128]{0:T(128)S(1)} %get-tuple-element.13, s32[128]{0:T(128)S(1)} %get-tuple-element.9), kind=kOutput, calls=%fused_computation.12 | convolution fusion | flops 269549568 | bytes 4719616 | tf_op jit(solution)/shard_map/dot_general | solution.py:14
  254.2 1.3 fusion.18
  (10 shorter events, 0.1 us)
Async XLA Ops:
  7.2 0.8 copy-start.6
  7.2 2.2 copy-start
  7.2 2.4 copy-start.5
  7.2 103.8 %all-gather.2.cloned.1.call-start = ((), (), s32[]{:S(2)}) async-start(), calls=%async_computation.3 | async-start | bytes 10485760 | tf_op jit(solution)/shard_map/all_gather | solution.py:41
  12.1 7.3 %copy-start.7 = (f32[128,2]{0,1:T(2,128)S(1)}, f32[128,2]{0,1:T(2,128)}, u32[]{:S(2)}) copy-start(f32[128,2]{0,1:T(2,128)} %param.12) | copy-start | bytes 3076
  12.1 7.6 %copy-start.4 = (bf16[128,2048]{1,0:T(8,128)(2,1)S(1)}, bf16[128,2048]{1,0:T(8,128)(2,1)}, u32[]{:S(2)}) copy-start(bf16[128,2048]{1,0:T(8,128)(2,1)} %param.13) | copy-start | bytes 1572868
  12.1 60.3 %all-to-all-start = ((bf16[32,16,2176]{2,1,0:T(8,128)(2,1)}), bf16[32,16,2176]{2,1,0:T(8,128)(2,1)S(1)}, u32[]{:S(2)}, u32[]{:S(2)}) async-start(bf16[32,16,2176]{2,1,0:T(8,128)(2,1)} %bitcast.2), calls=%async_computation | async-start | bytes 4456448 | tf_op jit(solution)/shard_map/all_to_all | solution.py:21
  72.4 1.4 copy-start.1
  73.8 53.6 %all-to-all-start.1 = ((bf16[32,16,2048]{2,1,0:T(8,128)(2,1)}), bf16[32,16,2048]{2,1,0:T(8,128)(2,1)S(1)}, u32[]{:S(2)}, u32[]{:S(2)}) async-start(bf16[32,16,2048]{2,1,0:T(8,128)(2,1)} %bitcast.4), calls=%async_computation.1 | async-start | bytes 4194304 | tf_op jit(solution)/shard_map/all_to_all | solution.py:21
  111.0 8.7 %copy-start.8 = (bf16[1024,2048]{1,0:T(8,128)(2,1)S(1)}, bf16[1024,2048]{1,0:T(8,128)(2,1)}, u32[]{:S(2)}) copy-start(bf16[1024,2048]{1,0:T(8,128)(2,1)} %param.10) | copy-start | bytes 12582916
  119.7 2.6 %copy-start.10 = (bf16[512,2048]{1,0:T(8,128)(2,1)}, bf16[512,2048]{1,0:T(8,128)(2,1)S(1)}, u32[]{:S(2)}) copy-start(bf16[512,2048]{1,0:T(8,128)(2,1)S(1)} %convolution_convert_fusion.3) | copy-start | bytes 6291460
  122.3 1.3 copy-start.2
  127.4 6.5 %copy-start.9 = (bf16[1024,2048]{1,0:T(8,128)(2,1)S(1)}, bf16[1024,2048]{1,0:T(8,128)(2,1)}, u32[]{:S(2)}) copy-start(bf16[1024,2048]{1,0:T(8,128)(2,1)} %param.10) | copy-start | bytes 12582916
  133.0 1.0 copy-start.12
  133.9 2.4 copy-start.3
  138.8 102.9 %all-to-all-start.2 = ((bf16[32,16,4096]{2,1,0:T(8,128)(2,1)}), bf16[32,16,4096]{2,1,0:T(8,128)(2,1)}, u32[]{:S(2)}, u32[]{:S(2)}) async-start(bf16[32,16,4096]{2,1,0:T(8,128)(2,1)} %bitcast.23), calls=%async_computation.2 | async-start | bytes 8388608 | tf_op jit(solution)/shard_map/all_to_all | solution.py:21
  145.9 4.3 %copy-start.11 = (bf16[512,2048]{1,0:T(8,128)(2,1)S(1)}, bf16[512,2048]{1,0:T(8,128)(2,1)}, u32[]{:S(2)}) copy-start(bf16[512,2048]{1,0:T(8,128)(2,1)} %copy-done.10) | copy-start | bytes 6291460
  145.9 4.3 %copy-start.13 = (bf16[512,1024]{1,0:T(8,128)(2,1)S(1)}, bf16[512,1024]{1,0:T(8,128)(2,1)}, u32[]{:S(2)}) copy-start(bf16[512,1024]{1,0:T(8,128)(2,1)} %copy-done.12) | copy-start | bytes 3145732
Sparse Core Ops, SparseCore 0:
  9.6 101.3 all-gather.1
